TPU v7x, 128 devices: a whole 4x4x4 slice. The times are simulated.
128 devices in a mesh: pair: 8 (over y, core), row: 16 (over z, x).
Axes of the slice: x: 4, y: 4, z: 4, core: 2. Of those that a mesh axis runs over, the one named last changes fastest.
Arguments:
- matrix: float32 [8192, 8192], P('row', 'pair'), may hold values from -12 to 12
- sources: int32 [3, 32], replicated, may hold values from 0 to 31, as said below
Outputs:
- rotated_matrix: float32 [8192, 8192], P('row', 'pair')
Inputs may be any that keep to these rules, and one draw needn't show every extreme that they name: `sources`: each round's row is a permutation of the slots. A slot's source lies on its own index of pair or on the next lower or higher one (slots per index: 4); for each index at most one slot draws from the lower neighbour and at most one from the higher one, with no wrap.
All inputs are finite; a program needn't handle non-finite values.
Results may differ from a plain program's by a relative error of at most 0.00016.
Values sent between devices are 32-bit elements; how exact they have to be, the bound alone decides.
No kernel may reach another device: no remote copies, remote signals or barrier semaphores. Data moves between devices by JAX's collectives and lax.ppermute only.
A program may use at most 320 MiB of HBM per device.

v0:
```python
from functools import partial

import jax
import jax.numpy as jnp
from jax import lax
from jax.experimental import pallas as pl
from jax.experimental.pallas import tpu as pltpu
from jax.sharding import PartitionSpec as P

BLOCK = 256
PAIR = 2 * BLOCK
ROUNDS = 3
UNROLLED = (0, 1, 2)
F32 = jnp.float32
BF16 = jnp.bfloat16
POLY = (2.25, -2.4375, 1.6875, -0.5625, 0.0625)

VMEM = pl.BlockSpec(memory_space=pltpu.VMEM)
SMEM = pl.BlockSpec(memory_space=pltpu.SMEM)
ANY = pl.BlockSpec(memory_space=pl.ANY)


def call(kernel, out_shape, in_specs, scratch=(), flops=0, mib=10, out_spec=VMEM, alias=None):
    return pl.pallas_call(
        kernel,
        out_shape=out_shape,
        in_specs=in_specs,
        out_specs=jax.tree.map(lambda _: out_spec, out_shape),
        scratch_shapes=list(scratch),
        input_output_aliases=alias or {},
        compiler_params=pltpu.CompilerParams(vmem_limit_bytes=mib * 1024 * 1024),
        cost_estimate=pl.CostEstimate(flops=flops, bytes_accessed=4_000_000, transcendentals=0),
    )


def split(x):
    high = x.astype(BF16)
    return high, (x - high.astype(F32)).astype(BF16)


def dot(a, b):
    return jnp.dot(a, b, preferred_element_type=F32)


def dot_t(a, b):
    return lax.dot_general(a, b, (((0,), (0,)), ((), ())), preferred_element_type=F32)


def product(ah, al, bh, bl, cols, mul=dot):
    return mul(ah[...], bh[:, cols]) + (mul(ah[...], bl[:, cols]) + mul(al[...], bh[:, cols]))


def eye_mask(n):
    return lax.broadcasted_iota(jnp.int32, (n, n), 0) == lax.broadcasted_iota(jnp.int32, (n, n), 1)


def upper_mask(n):
    return lax.broadcasted_iota(jnp.int32, (n, n), 0) < lax.broadcasted_iota(jnp.int32, (n, n), 1)


def own_source(src_ref, dev_ref, round_index, slot, slots):
    base = dev_ref[0] * slots
    return src_ref[round_index, base + slot] - base


def leaving(src_ref, dev_ref, round_index, step, slots):
    base = dev_ref[0] * slots
    last = src_ref.shape[1] - slots
    there = jnp.clip(base + step * slots, 0, last)
    found = jnp.int32(0)
    for slot in range(slots):
        offset = src_ref[round_index, there + slot] - base
        found = jnp.where((offset >= 0) & (offset < slots), offset, found)
    return found


def picked(offset, slots, own_ref, lower_ref, upper_ref):
    own = own_ref[jnp.clip(offset, 0, slots - 1)]
    return jnp.where(offset < 0, lower_ref[...], jnp.where(offset >= slots, upper_ref[...], own))


def first_gram(a_ref, part_ref, high_ref, low_ref):
    pairs = a_ref.shape[1] // PAIR
    chunks = part_ref.shape[0]
    rows = part_ref.shape[1] - 8
    per = BLOCK // rows
    part_ref[:, rows:, :] = jnp.zeros((chunks, 8, BLOCK), F32)
    for p in range(pairs):
        one, two = pl.ds(p * PAIR, BLOCK), pl.ds(p * PAIR + BLOCK, BLOCK)
        for cols in (one, two):
            high_ref[:, cols], low_ref[:, cols] = split(a_ref[:, cols])

        def gram(x, y):
            return dot_t(high_ref[:, x], high_ref[:, y]) + (
                dot_t(high_ref[:, x], low_ref[:, y]) + dot_t(low_ref[:, x], high_ref[:, y])
            )

        cross = gram(one, two)
        first = gram(one, one)
        second = gram(two, two)
        eye = eye_mask(BLOCK)
        diagonal = jnp.sum(jnp.where(eye, second, 0.0), axis=0, keepdims=True)
        both = jnp.where(eye | upper_mask(BLOCK), first, second)
        start = 2 * per * p
        for j in range(per):
            part_ref[start + j, :rows, :] = cross[j * rows:(j + 1) * rows]
            part_ref[start + per + j, :rows, :] = both[j * rows:(j + 1) * rows]
        part_ref[start, rows:, :] = jnp.broadcast_to(diagonal, (8, BLOCK))


def cross_gram(round_index, slots, src_ref, dev_ref, own_ref, lower_ref, upper_ref, part_ref, high_ref, low_ref):
    rows = part_ref.shape[1]
    per = BLOCK // rows
    for slot in range(slots):
        offset = own_source(src_ref, dev_ref, round_index, slot, slots)
        high, low = split(picked(offset, slots, own_ref, lower_ref, upper_ref))
        high_ref[:, pl.ds(slot * BLOCK, BLOCK)] = high
        low_ref[:, pl.ds(slot * BLOCK, BLOCK)] = low
    for p in range(slots // 2):
        one, two = pl.ds(p * PAIR, BLOCK), pl.ds(p * PAIR + BLOCK, BLOCK)
        cross = dot_t(high_ref[:, one], high_ref[:, two]) + (
            dot_t(high_ref[:, one], low_ref[:, two]) + dot_t(low_ref[:, one], high_ref[:, two])
        )
        for j in range(per):
            part_ref[p * per + j] = cross[j * rows:(j + 1) * rows]


def set_generator(total_rows, cross, first, second, kf, kh, kl):
    eye = eye_mask(BLOCK)
    sign = jnp.where(eye, 0.0, jnp.where(upper_mask(BLOCK), 1.0, -1.0))
    scale = 1.0 / total_rows
    roots = []
    for block in (first, second):
        kept = jnp.where(eye, block * scale, 0.0)
        roots.append(
            (
                lax.rsqrt(jnp.sum(kept, axis=1, keepdims=True) + 1e-06),
                lax.rsqrt(jnp.sum(kept, axis=0, keepdims=True) + 1e-06),
            )
        )
    k11 = first * scale * roots[0][0] * roots[0][1] * sign
    k22 = second * scale * roots[1][0] * roots[1][1] * sign
    k12 = cross * scale * roots[0][0] * roots[1][1]
    total = jnp.sum(k11 * k11 + k22 * k22 + 2.0 * (k12 * k12), keepdims=True)
    lo, hi = pl.ds(0, BLOCK), pl.ds(BLOCK, BLOCK)
    for r, c, block in ((lo, lo, k11), (lo, hi, k12), (hi, lo, -k12.T), (hi, hi, k22)):
        kf[r, c] = block
        high, low = split(block)
        kh[r, c] = high
        kl[r, c] = low
    return 1.0 / (1.0 + jnp.sqrt(total))


def rotations(pairs, generator, works, out_high, out_low):
    part = [pl.ds(0, BLOCK), pl.ds(BLOCK, BLOCK)]
    upper = ((0, 0), (0, 1), (1, 1))
    held = [{} for _ in works]

    def turn(p):
        return p if len(works) == pairs else 0

    def start(p):
        c = generator(p, works[turn(p)])
        u = c * c
        b0, b1, b2, b3, b4 = POLY
        held[turn(p)]["c"] = c
        held[turn(p)]["k"] = (
            u,
            b0 + u * (b1 + u * (b2 + u * (b3 + u * b4))),
            b1 + u * (2 * b2 + u * (3 * b3 + u * 4 * b4)),
            b2 + u * (3 * b3 + u * 6 * b4),
            b3 + u * 4 * b4,
            b4,
        )

    def block(ah, al, bh, bl, i, j):
        r, c = part[i], part[j]
        return dot(ah[r, :], bh[:, c]) + (dot(ah[r, :], bl[:, c]) + dot(al[r, :], bh[:, c]))

    def put(high, low, i, j, value):
        high[part[i], part[j]], low[part[i], part[j]] = split(value)

    def put_symmetric(high, low, i, j, value):
        put(high, low, i, j, value)
        if i != j:
            put(high, low, j, i, value.T)

    def square(p):
        kf, kh, kl, sf, sh, sl, vf, vh, vl, th, tl, xh, xl, yh, yl = works[turn(p)]
        for i, j in upper:
            s = -held[turn(p)]["k"][0] * block(kh, kl, kh, kl, i, j)
            sf[part[i], part[j]] = s
            put_symmetric(sh, sl, i, j, s)

    def fourth(p):
        kf, kh, kl, sf, sh, sl, vf, vh, vl, th, tl, xh, xl, yh, yl = works[turn(p)]
        u, a0, a1, a2, a3, a4 = held[turn(p)]["k"]
        for i, j in upper:
            v = block(sh, sl, sh, sl, i, j)
            vf[part[i], part[j]] = v
            put_symmetric(vh, vl, i, j, v)
            put_symmetric(th, tl, i, j, a3 * sf[part[i], part[j]] + a4 * v)

    def polynomial(p):
        kf, kh, kl, sf, sh, sl, vf, vh, vl, th, tl, xh, xl, yh, yl = works[turn(p)]
        u, a0, a1, a2, a3, a4 = held[turn(p)]["k"]
        for i, j in upper:
            t = a1 * sf[part[i], part[j]] + a2 * vf[part[i], part[j]] + block(vh, vl, th, tl, i, j)
            vf[part[i], part[j]] = t
            put_symmetric(sh, sl, i, j, t)

    def second(p):
        kf, kh, kl, sf, sh, sl, vf, vh, vl, th, tl, xh, xl, yh, yl = works[turn(p)]
        u, a0, a1, a2, a3, a4 = held[turn(p)]["k"]
        c = held[turn(p)]["c"]
        for i, j in upper:
            odd = a0 * kf[part[i], part[j]] + block(kh, kl, sh, sl, i, j)
            even = vf[part[i], part[j]]
            if i == j:
                even = jnp.where(eye_mask(BLOCK), even + a0, even)
            x, y = c * (even - odd), c * (even + odd)
            sf[part[i], part[j]] = x
            put(xh, xl, i, j, x)
            put(yh, yl, i, j, y)
            if i != j:
                turned = y.T
                sf[part[j], part[i]] = turned
                put(xh, xl, j, i, turned)
                put(yh, yl, j, i, x.T)

    def metric(p):
        kf, kh, kl, sf, sh, sl, vf, vh, vl, th, tl, xh, xl, yh, yl = works[turn(p)]
        for i, j in upper:
            put_symmetric(vh, vl, i, j, block(yh, yl, xh, xl, i, j))

    def third(p):
        kf, kh, kl, sf, sh, sl, vf, vh, vl, th, tl, xh, xl, yh, yl = works[turn(p)]
        for cols in part:
            r = 1.5 * sf[:, cols] - 0.5 * product(xh, xl, vh, vl, cols)
            out_high[p, :, cols], out_low[p, :, cols] = split(r)

    stages = (start, square, fourth, polynomial, second, metric, third)
    if len(works) == pairs:
        for step in range(len(stages) + pairs - 1):
            for p in range(pairs):
                if 0 <= step - p < len(stages):
                    stages[step - p](p)
    else:

        @pl.loop(0, pairs)
        def _(p):
            for stage in stages:
                stage(p)


def leave(round_index, slots, src_ref, dev_ref, high_ref, low_ref, rh_ref, rl_ref, right_ref, left_ref):
    for step, out_ref in ((1, right_ref), (-1, left_ref)):
        slot = leaving(src_ref, dev_ref, round_index, step, slots)
        pair, half = slot >> 1, slot & 1
        rows = pl.ds(pl.multiple_of(pair * PAIR, PAIR), PAIR)
        cols = pl.ds(pl.multiple_of(half * BLOCK, BLOCK), BLOCK)
        out_ref[...] = product(
            high_ref.at[:, rows], low_ref.at[:, rows], rh_ref.at[pair], rl_ref.at[pair], cols
        )


def first_rotate(total_rows, slots, src_ref, dev_ref, sum_ref, high_ref, low_ref,
                 right_ref, left_ref, rh_ref, rl_ref, gh_ref, gl_ref, *rest):
    rows = sum_ref.shape[1] - 8
    per = BLOCK // rows
    works = [rest[at:at + 15] for at in range(0, len(rest), 15)]
    lo, hi = pl.ds(0, BLOCK), pl.ds(BLOCK, BLOCK)

    def generator(p, work):
        first_chunk = 2 * per * p
        cross = sum_ref[pl.ds(first_chunk, per), :rows, :].reshape(BLOCK, BLOCK)
        both = sum_ref[pl.ds(first_chunk + per, per), :rows, :].reshape(BLOCK, BLOCK)
        diagonal = sum_ref[first_chunk, rows:rows + 1, :]
        turned = both.T
        eye, upper = eye_mask(BLOCK), upper_mask(BLOCK)
        first = jnp.where(eye | upper, both, turned)
        second = jnp.where(eye, diagonal, jnp.where(upper, turned, both))
        for r, c, block in ((lo, lo, first), (lo, hi, cross), (hi, lo, cross.T), (hi, hi, second)):
            high, low = split(block)
            gh_ref[p, r, c] = high
            gl_ref[p, r, c] = low
        return set_generator(total_rows, cross, first, second, *work[:3])

    rotations(slots // 2, generator, works, rh_ref, rl_ref)
    leave(0, slots, src_ref, dev_ref, high_ref, low_ref, rh_ref, rl_ref, right_ref, left_ref)


def later_rotate(round_index, last, total_rows, slots, src_ref, dev_ref, sum_ref, self_ref,
                 high_ref, low_ref, right_ref, left_ref, rh_ref, rl_ref, *rest):
    rows = sum_ref.shape[1]
    per = BLOCK // rows
    if not last:
        gh_ref, gl_ref = rest[:2]
    rest = rest if last else rest[2:]
    works = [rest[at:at + 15] for at in range(0, len(rest), 15)]
    lo, hi = pl.ds(0, BLOCK), pl.ds(BLOCK, BLOCK)

    def generator(p, work):
        cross = sum_ref[pl.ds(p * per, per)].reshape(BLOCK, BLOCK)
        first, second = self_ref[2 * p], self_ref[2 * p + 1]
        if not last:
            for r, c, block in ((lo, lo, first), (lo, hi, cross), (hi, lo, cross.T), (hi, hi, second)):
                high, low = split(block)
                gh_ref[p, r, c] = high
                gl_ref[p, r, c] = low
        return set_generator(total_rows, cross, first, second, *work[:3])

    rotations(slots // 2, generator, works, rh_ref, rl_ref)
    leave(round_index, slots, src_ref, dev_ref, high_ref, low_ref, rh_ref, rl_ref, right_ref, left_ref)


def carry_self(round_index, slots, src_ref, dev_ref, gh_ref, gl_ref, rh_ref, rl_ref,
               self_ref, right_ref, left_ref, *work):
    @pl.loop(0, slots // 2)
    def _(p):
        for half in range(2):
            cols = pl.ds(half * BLOCK, BLOCK)
            yh, yl = work[2 * half:2 * half + 2]
            yh[...], yl[...] = split(product(gh_ref.at[p], gl_ref.at[p], rh_ref.at[p], rl_ref.at[p], cols))
        for half in range(2):
            cols = pl.ds(half * BLOCK, BLOCK)
            yh, yl = work[2 * half:2 * half + 2]
            self_ref[2 * p + half] = dot_t(rh_ref[p, :, cols], yh[...]) + (
                dot_t(rh_ref[p, :, cols], yl[...]) + dot_t(rl_ref[p, :, cols], yh[...])
            )

    right_ref[...] = self_ref[leaving(src_ref, dev_ref, round_index, 1, slots)]
    left_ref[...] = self_ref[leaving(src_ref, dev_ref, round_index, -1, slots)]


def take_self(round_index, slots, src_ref, dev_ref, self_ref, lower_ref, upper_ref, after_ref, out_ref):
    for slot in range(slots):
        offset = own_source(src_ref, dev_ref, round_index, slot, slots)
        out_ref[slot] = picked(offset, slots, self_ref, lower_ref, upper_ref)


def apply(slots, high_ref, low_ref, rh_ref, rl_ref, after_ref, own_ref):
    @pl.loop(0, slots // 2)
    def _(p):
        rows = pl.ds(pl.multiple_of(p * PAIR, PAIR), PAIR)
        for half in range(2):
            own_ref[2 * p + half] = product(
                high_ref.at[:, rows], low_ref.at[:, rows], rh_ref.at[p], rl_ref.at[p], pl.ds(half * BLOCK, BLOCK)
            )


def apply_last(round_index, slots, src_ref, dev_ref, high_ref, low_ref, rh_ref, rl_ref, out_ref, own_ref, sems):
    apply(slots, high_ref, low_ref, rh_ref, rl_ref, None, own_ref)
    offsets = [own_source(src_ref, dev_ref, round_index, slot, slots) for slot in range(slots)]
    for wait in (False, True):
        for slot, offset in enumerate(offsets):
            @pl.when((offset >= 0) & (offset < slots))
            def _():
                kept = own_ref.at[jnp.clip(offset, 0, slots - 1)]
                goal = out_ref.at[:, pl.ds(slot * BLOCK, BLOCK)]
                copy = pltpu.make_async_copy(kept, goal, sems.at[slot])
                copy.wait() if wait else copy.start()


def settle(round_index, slots, src_ref, dev_ref, most_ref, lower_ref, upper_ref, out_ref, sems):
    offsets = [own_source(src_ref, dev_ref, round_index, slot, slots) for slot in range(slots)]
    for wait in (False, True):
        for slot, offset in enumerate(offsets):
            goal = out_ref.at[:, pl.ds(slot * BLOCK, BLOCK)]

            @pl.when(offset < 0)
            def _():
                copy = pltpu.make_async_copy(lower_ref, goal, sems.at[slot])
                copy.wait() if wait else copy.start()

            @pl.when(offset >= slots)
            def _():
                copy = pltpu.make_async_copy(upper_ref, goal, sems.at[slot])
                copy.wait() if wait else copy.start()


def to_next(x, by):
    count = lax.axis_size("pair")
    return lax.ppermute(x, "pair", [(i, (i + by) % count) for i in range(count)])


def add_up(pieces_ref, out_ref):
    total = jnp.sum(pieces_ref[...], axis=0)
    for chunk in range(out_ref.shape[0]):
        out_ref[chunk] = total


def sum_rows(part):
    pieces = lax.all_to_all(part, "row", 0, 0, tiled=True)
    mine = call(add_up, jax.ShapeDtypeStruct(part.shape, F32), [VMEM])(pieces)
    return lax.all_to_all(mine, "row", 0, 0, tiled=True)


def body(matrix, sources):
    rows, columns = matrix.shape
    slots = columns // BLOCK
    pairs = slots // 2
    row_count = lax.axis_size("row")
    total_rows = rows * row_count
    device = lax.axis_index("pair").astype(jnp.int32).reshape(1)
    f32 = partial(jax.ShapeDtypeStruct, dtype=F32)
    bf16 = partial(jax.ShapeDtypeStruct, dtype=BF16)
    square = (PAIR, PAIR)
    f, h = pltpu.VMEM(square, F32), pltpu.VMEM(square, BF16)
    work = [f, h, h, f, h, h, f, h, h, h, h, h, h, h, h]
    product_flops = 2 * PAIR**3 * 3
    sems = pltpu.SemaphoreType.DMA((slots,))
    part, high, low = call(
        first_gram,
        (f32((row_count, 2 * slots * BLOCK // 2 // row_count + 8, BLOCK)), bf16(matrix.shape), bf16(matrix.shape)),
        [VMEM],
        flops=3 * pairs * product_flops // 4,
    )(matrix)
    part, sources, device = lax.optimization_barrier((part, sources, device))
    block, small = f32((rows, BLOCK)), f32((BLOCK, BLOCK))
    carried = ()
    for index in range(ROUNDS):
        last = index == ROUNDS - 1
        summed = sum_rows(part)
        kernel = first_rotate if index == 0 else partial(later_rotate, index, last)
        right, left, rh, rl, *gram = call(
            partial(kernel, total_rows, slots),
            (block, block) + (bf16((pairs,) + square),) * (2 if last else 4),
            [SMEM, SMEM] + [VMEM] * (3 + len(carried)),
            work * (pairs if index in UNROLLED else 1),
            flops=7 * pairs * product_flops,
            mib=20,
        )(sources, device, summed, *carried, high, low)
        lower, upper = to_next(right, 1), to_next(left, -1)
        if last:
            most = call(
                partial(apply_last, index, slots),
                f32(matrix.shape),
                [SMEM, SMEM] + [VMEM] * 4,
                [pltpu.VMEM((slots, rows, BLOCK), F32), sems],
                flops=pairs * product_flops,
                out_spec=ANY,
            )(sources, device, high, low, rh, rl)
            return call(
                partial(settle, index, slots),
                f32(matrix.shape),
                [SMEM, SMEM, ANY, VMEM, VMEM],
                [sems],
                out_spec=ANY,
                alias={2: 0},
            )(sources, device, most, lower, upper)
        selves, self_right, self_left = call(
            partial(carry_self, index, slots),
            (f32((slots, BLOCK, BLOCK)), small, small),
            [SMEM, SMEM] + [VMEM] * 4,
            [pltpu.VMEM((PAIR, BLOCK), BF16)] * 4,
            flops=3 * pairs * product_flops // 2,
        )(sources, device, *gram, rh, rl)
        own = call(
            partial(apply, slots),
            f32((slots, rows, BLOCK)),
            [VMEM] * 4 + [ANY],
            flops=pairs * product_flops,
        )(high, low, rh, rl, selves)
        lower_self, upper_self = to_next(self_right, 1), to_next(self_left, -1)
        part, high, low = call(
            partial(cross_gram, index, slots),
            (f32((row_count, pairs * BLOCK // row_count, BLOCK)), bf16(matrix.shape), bf16(matrix.shape)),
            [SMEM, SMEM] + [VMEM] * 3,
            flops=pairs * product_flops // 4,
        )(sources, device, own, lower, upper)
        selves = call(
            partial(take_self, index, slots), f32((slots, BLOCK, BLOCK)), [SMEM, SMEM] + [VMEM] * 3 + [ANY]
        )(sources, device, selves, lower_self, upper_self, part)
        part, *carried = lax.optimization_barrier((part, selves))


def solution(mesh):
    placed = (P("row", "pair"), P())
    return jax.shard_map(
        body, mesh=mesh, in_specs=placed, out_specs=P("row", "pair"), check_vma=False
    )
```

profile of v0, /device:TPU:1, one launch (start us, length us, event | category | flops | bytes accessed | tf_op | source)
XLA Modules:
  0.0 179.7 jit_solution(9122774737156363635)
XLA Ops:
  0.0 1.6 copy-done.1
  3.1 25.6 %all_to_all.30.pieces_ref = f32[16,72,256]{2,1,0:T(8,128)S(1)} all-to-all(f32[16,72,256]{2,1,0:T(8,128)S(1)} %get-tuple-element.48), channel_id=1, replica_groups=mesh['pair'=8,'row'=16] {'row'}, dimensions={0} | all-to-all | bytes 2359296 | tf_op jit(solution)/shard_map/all_to_all | solution.py:394
  28.9 19.8 %all_to_all.31.sum_ref = f32[16,72,256]{2,1,0:T(8,128)S(1)} all-to-all(f32[16,72,256]{2,1,0:T(8,128)S(1)} %shard_map.29), channel_id=1, replica_groups=mesh['pair'=8,'row'=16] {'row'}, dimensions={0} | all-to-all | bytes 2359296 | tf_op jit(solution)/shard_map/all_to_all | solution.py:396
  48.7 10.4 %shard_map.30 = (f32[512,256]{1,0:T(8,128)S(1)}, f32[512,256]{1,0:T(8,128)S(1)}, bf16[2,512,512]{2,1,0:T(8,128)(2,1)S(1)}, bf16[2,512,512]{2,1,0:T(8,128)(2,1)S(...) custom-call(s32[3,32]{1,0:T(4,128)S(1)} %copy-done, s32[1]{0:T(128)} %bitcast.dev_ref, ...), custom_call_target="tpu_custom_call" | custom-call | flops 11274289152 | bytes 4000000 | tf_op jit(solution)/shard_map/pallas_call | solution.py:426
  59.1 4.2 %collective-permute-start = (f32[512,256]{1,0:T(8,128)S(1)}, f32[512,256]{1,0:T(8,128)S(1)}, u32[]{:S(2)}, u32[]{:S(2)}) collective-permute-start(f32[512,256]{1,0:T(8,128)S(1)} %get-tuple-element.54), channel_id=1, source_target_pairs={{0,16},{16,32},{32,48},{48,64},{64,80},{80,96},{96,112},{112,0},{1... | collective-permute-start | bytes 1572872 | tf_op jit(solution)/shard_map/ppermute | solution.py:384
  63.3 3.5 %shard_map.31 = (f32[4,256,256]{2,1,0:T(8,128)S(1)}, f32[256,256]{1,0:T(8,128)S(1)}, f32[256,256]{1,0:T(8,128)S(1)}) custom-call(s32[3,32]{1,0:T(4,128)S(1)} %copy-done, s32[1]{0:T(128)} %bitcast.dev_ref, bf16[2,512,512]{2,1,0:T(8,128)(2,1)S(1)} %get-tuple-element.51.gh_ref, bf16[2,512,512]{2,1,0:T(8,128)(2,1)S(1)} %get-tuple-element.52.gl_ref, ...), custom_call_target="tpu_custom_call" | custom-call | flops 2415919104 | bytes 4000000 | tf_op jit(solution)/shard_map/pallas_call | solution.py:452
  66.9 1.8 collective-permute-start.2
  68.7 1.9 %shard_map.32.own_ref = f32[4,512,256]{2,1,0:T(8,128)S(1)} custom-call(bf16[512,1024]{1,0:T(8,128)(2,1)S(1)} %get-tuple-element.46.high_ref, bf16[512,1024]{1,0:T(8,128)(2,1)S(1)} %get-tuple-element.47.low_ref, bf16[2,512,512]{2,1,0:T(8,128)(2,1)S(1)} %get-tuple-element.49.rh_ref, bf16[2,512,512]{2,1,0:T(8,128)(2,1)S(1)} %get-tuple-element.50.rl_ref, ...), custom_call_target="tpu_custom_call" | custom-call | flops 1610612736 | bytes 4000000 | tf_op jit(solution)/shard_map/pallas_call | solution.py:459
  73.4 1.6 collective-permute-done.3.upper_ref
  75.8 13.2 %all_to_all.32.pieces_ref = f32[16,32,256]{2,1,0:T(8,128)S(1)} all-to-all(f32[16,32,256]{2,1,0:T(8,128)S(1)} %get-tuple-element.61.after_ref), channel_id=1, replica_groups=mesh['pair'=8,'row'=16] {'row'}, dimensions={0} | all-to-all | bytes 1048576 | tf_op jit(solution)/shard_map/all_to_all | solution.py:394
  89.0 13.4 %all_to_all.33.sum_ref = f32[16,32,256]{2,1,0:T(8,128)S(1)} all-to-all(f32[16,32,256]{2,1,0:T(8,128)S(1)} %shard_map.35), channel_id=1, replica_groups=mesh['pair'=8,'row'=16] {'row'}, dimensions={0} | all-to-all | bytes 1048576 | tf_op jit(solution)/shard_map/all_to_all | solution.py:396
  102.4 10.3 %shard_map.36 = (f32[512,256]{1,0:T(8,128)S(1)}, f32[512,256]{1,0:T(8,128)S(1)}, bf16[2,512,512]{2,1,0:T(8,128)(2,1)S(1)}, bf16[2,512,512]{2,1,0:T(8,128)(2,1)S(...) custom-call(s32[3,32]{1,0:T(4,128)S(1)} %copy-done, s32[1]{0:T(128)} %bitcast.dev_ref, ...), custom_call_target="tpu_custom_call" | custom-call | flops 11274289152 | bytes 4000000 | tf_op jit(solution)/shard_map/pallas_call | solution.py:426
  112.8 3.7 %collective-permute-start.4 = (f32[512,256]{1,0:T(8,128)S(1)}, f32[512,256]{1,0:T(8,128)S(1)}, u32[]{:S(2)}, u32[]{:S(2)}) collective-permute-start(f32[512,256]{1,0:T(8,128)S(1)} %get-tuple-element.68), channel_id=1, source_target_pairs={{0,16},{16,32},{32,48},{48,64},{64,80},{80,96},{96,112},{112,0},{1... | collective-permute-start | bytes 1572872 | tf_op jit(solution)/shard_map/ppermute | solution.py:384
  116.5 3.5 %shard_map.37 = (f32[4,256,256]{2,1,0:T(8,128)S(1)}, f32[256,256]{1,0:T(8,128)S(1)}, f32[256,256]{1,0:T(8,128)S(1)}) custom-call(s32[3,32]{1,0:T(4,128)S(1)} %copy-done, s32[1]{0:T(128)} %bitcast.dev_ref, bf16[2,512,512]{2,1,0:T(8,128)(2,1)S(1)} %get-tuple-element.65.gh_ref, bf16[2,512,512]{2,1,0:T(8,128)(2,1)S(1)} %get-tuple-element.66.gl_ref, ...), custom_call_target="tpu_custom_call" | custom-call | flops 2415919104 | bytes 4000000 | tf_op jit(solution)/shard_map/pallas_call | solution.py:452
  120.0 1.8 collective-permute-start.6
  121.7 1.9 %shard_map.38.own_ref = f32[4,512,256]{2,1,0:T(8,128)S(1)} custom-call(bf16[512,1024]{1,0:T(8,128)(2,1)S(1)} %get-tuple-element.56.high_ref, bf16[512,1024]{1,0:T(8,128)(2,1)S(1)} %get-tuple-element.57.low_ref, bf16[2,512,512]{2,1,0:T(8,128)(2,1)S(1)} %get-tuple-element.63.rh_ref, bf16[2,512,512]{2,1,0:T(8,128)(2,1)S(1)} %get-tuple-element.64.rl_ref, ...), custom_call_target="tpu_custom_call" | custom-call | flops 1610612736 | bytes 4000000 | tf_op jit(solution)/shard_map/pallas_call | solution.py:459
  126.5 1.6 collective-permute-done.7.upper_ref
  128.9 13.2 %all_to_all.34.pieces_ref = f32[16,32,256]{2,1,0:T(8,128)S(1)} all-to-all(f32[16,32,256]{2,1,0:T(8,128)S(1)} %get-tuple-element.75.after_ref), channel_id=1, replica_groups=mesh['pair'=8,'row'=16] {'row'}, dimensions={0} | all-to-all | bytes 1048576 | tf_op jit(solution)/shard_map/all_to_all | solution.py:394
  142.2 13.4 %all_to_all.35.sum_ref = f32[16,32,256]{2,1,0:T(8,128)S(1)} all-to-all(f32[16,32,256]{2,1,0:T(8,128)S(1)} %shard_map.41), channel_id=1, replica_groups=mesh['pair'=8,'row'=16] {'row'}, dimensions={0} | all-to-all | bytes 1048576 | tf_op jit(solution)/shard_map/all_to_all | solution.py:396
  155.6 10.2 %shard_map.42 = (f32[512,256]{1,0:T(8,128)S(1)}, f32[512,256]{1,0:T(8,128)S(1)}, bf16[2,512,512]{2,1,0:T(8,128)(2,1)S(1)}, bf16[2,512,512]{2,1,0:T(8,128)(2,1)S(1)}) custom-call(s32[3,32]{1,0:T(4,128)S(1)} %copy-done, s32[1]{0:T(128)} %bitcast.dev_ref, f32[16,32,256]{2,1,0:T(8,128)S(1)} %all_to_all.35.sum_ref, f32[4,256,256]{2,1,0:T(8,128)S(1)} %shard_map.40.self_ref, ...), custom_call_target="tpu_custom_call" | custom-call | flops 11274289152 | bytes 4000000 | tf_op jit(solution)/shard_map/pallas_call | solution.py:426
  165.9 3.4 %collective-permute-start.8 = (f32[512,256]{1,0:T(8,128)S(1)}, f32[512,256]{1,0:T(8,128)S(1)}, u32[]{:S(2)}, u32[]{:S(2)}) collective-permute-start(f32[512,256]{1,0:T(8,128)S(1)} %get-tuple-element.79), channel_id=1, source_target_pairs={{0,16},{16,32},{32,48},{48,64},{64,80},{80,96},{96,112},{112,0},{1... | collective-permute-start | bytes 1572872 | tf_op jit(solution)/shard_map/ppermute | solution.py:384
  169.3 3.5 %shard_map.43.most_ref = f32[512,1024]{1,0:T(8,128)} custom-call(s32[3,32]{1,0:T(4,128)S(1)} %copy-done, s32[1]{0:T(128)} %bitcast.dev_ref, bf16[512,1024]{1,0:T(8,128)(2,1)S(1)} %get-tuple-element.70.high_ref, bf16[512,1024]{1,0:T(8,128)(2,1)S(1)} %get-tuple-element.71.low_ref, bf16[2,512,512]{2,1,0:T(8,128)(2,1)S(1)} %get-tuple-element.77.rh_ref, ...), custom_call_target="tpu_custom_call" | custom-call | flops 1610612736 | bytes 4000000 | tf_op jit(solution)/shard_map/pallas_call | solution.py:436
  172.8 2.6 %collective-permute-done.8.lower_ref = f32[512,256]{1,0:T(8,128)S(1)} collective-permute-done((f32[512,256]{1,0:T(8,128)S(1)}, f32[512,256]{1,0:T(8,128)S(1)}, u32[]{:S(2)}, u32[]{:S(2)}) %collective-permute-start.8) | collective-permute-done | bytes 524320 | tf_op jit(solution)/shard_map/ppermute | solution.py:384
  175.4 2.5 %collective-permute-done.9.upper_ref = f32[512,256]{1,0:T(8,128)S(1)} collective-permute-done((f32[512,256]{1,0:T(8,128)S(1)}, f32[512,256]{1,0:T(8,128)S(1)}, u32[]{:S(2)}, u32[]{:S(2)}) %collective-permute-start.9) | collective-permute-done | bytes 524320 | tf_op jit(solution)/shard_map/ppermute | solution.py:384
  (23 shorter events, 10.4 us)
Async XLA Ops:
  0.0 1.6 copy-start.1
  28.8 19.9 %copy-start = (s32[3,32]{1,0:T(4,128)S(1)}, s32[3,32]{1,0:T(4,128)}, u32[]{:S(2)}) copy-start(s32[3,32]{1,0:T(4,128)} %src_ref.10) | copy-start | bytes 1156
  59.1 11.5 %collective-permute-start = (f32[512,256]{1,0:T(8,128)S(1)}, f32[512,256]{1,0:T(8,128)S(1)}, u32[]{:S(2)}, u32[]{:S(2)}) collective-permute-start(f32[512,256]{1,0:T(8,128)S(1)} %get-tuple-element.54), channel_id=1, source_target_pairs={{0,16},{16,32},{32,48},{48,64},{64,80},{80,96},{96,112},{112,0},{1... | collective-permute-start | bytes 1572872 | tf_op jit(solution)/shard_map/ppermute | solution.py:384
  63.3 8.6 %collective-permute-start.1 = (f32[512,256]{1,0:T(8,128)S(1)}, f32[512,256]{1,0:T(8,128)S(1)}, u32[]{:S(2)}, u32[]{:S(2)}) collective-permute-start(f32[512,256]{1,0:T(8,128)S(1)} %get-tuple-element.55), channel_id=1, source_target_pairs={{0,112},{16,0},{32,16},{48,32},{64,48},{80,64},{96,80},{112,96},{1... | collective-permute-start | bytes 1572872 | tf_op jit(solution)/shard_map/ppermute | solution.py:384
  66.9 6.6 %collective-permute-start.2 = (f32[256,256]{1,0:T(8,128)S(1)}, f32[256,256]{1,0:T(8,128)S(1)}, u32[]{:S(2)}, u32[]{:S(2)}) collective-permute-start(f32[256,256]{1,0:T(8,128)S(1)} %get-tuple-element.59), channel_id=1, source_target_pairs={{0,16},{16,32},{32,48},{48,64},{64,80},{80,96},{96,112},{112,0},{1... | collective-permute-start | bytes 786440 | tf_op jit(solution)/shard_map/ppermute | solution.py:384
  68.6 6.4 %collective-permute-start.3 = (f32[256,256]{1,0:T(8,128)S(1)}, f32[256,256]{1,0:T(8,128)S(1)}, u32[]{:S(2)}, u32[]{:S(2)}) collective-permute-start(f32[256,256]{1,0:T(8,128)S(1)} %get-tuple-element.60), channel_id=1, source_target_pairs={{0,112},{16,0},{32,16},{48,32},{64,48},{80,64},{96,80},{112,96},{1... | collective-permute-start | bytes 786440 | tf_op jit(solution)/shard_map/ppermute | solution.py:384
  112.8 10.9 %collective-permute-start.4 = (f32[512,256]{1,0:T(8,128)S(1)}, f32[512,256]{1,0:T(8,128)S(1)}, u32[]{:S(2)}, u32[]{:S(2)}) collective-permute-start(f32[512,256]{1,0:T(8,128)S(1)} %get-tuple-element.68), channel_id=1, source_target_pairs={{0,16},{16,32},{32,48},{48,64},{64,80},{80,96},{96,112},{112,0},{1... | collective-permute-start | bytes 1572872 | tf_op jit(solution)/shard_map/ppermute | solution.py:384
  116.4 8.6 %collective-permute-start.5 = (f32[512,256]{1,0:T(8,128)S(1)}, f32[512,256]{1,0:T(8,128)S(1)}, u32[]{:S(2)}, u32[]{:S(2)}) collective-permute-start(f32[512,256]{1,0:T(8,128)S(1)} %get-tuple-element.69), channel_id=1, source_target_pairs={{0,112},{16,0},{32,16},{48,32},{64,48},{80,64},{96,80},{112,96},{1... | collective-permute-start | bytes 1572872 | tf_op jit(solution)/shard_map/ppermute | solution.py:384
  120.0 6.6 %collective-permute-start.6 = (f32[256,256]{1,0:T(8,128)S(1)}, f32[256,256]{1,0:T(8,128)S(1)}, u32[]{:S(2)}, u32[]{:S(2)}) collective-permute-start(f32[256,256]{1,0:T(8,128)S(1)} %get-tuple-element.73), channel_id=1, source_target_pairs={{0,16},{16,32},{32,48},{48,64},{64,80},{80,96},{96,112},{112,0},{1... | collective-permute-start | bytes 786440 | tf_op jit(solution)/shard_map/ppermute | solution.py:384
  121.7 6.4 %collective-permute-start.7 = (f32[256,256]{1,0:T(8,128)S(1)}, f32[256,256]{1,0:T(8,128)S(1)}, u32[]{:S(2)}, u32[]{:S(2)}) collective-permute-start(f32[256,256]{1,0:T(8,128)S(1)} %get-tuple-element.74), channel_id=1, source_target_pairs={{0,112},{16,0},{32,16},{48,32},{64,48},{80,64},{96,80},{112,96},{1... | collective-permute-start | bytes 786440 | tf_op jit(solution)/shard_map/ppermute | solution.py:384
  165.9 9.6 %collective-permute-start.8 = (f32[512,256]{1,0:T(8,128)S(1)}, f32[512,256]{1,0:T(8,128)S(1)}, u32[]{:S(2)}, u32[]{:S(2)}) collective-permute-start(f32[512,256]{1,0:T(8,128)S(1)} %get-tuple-element.79), channel_id=1, source_target_pairs={{0,16},{16,32},{32,48},{48,64},{64,80},{80,96},{96,112},{112,0},{1... | collective-permute-start | bytes 1572872 | tf_op jit(solution)/shard_map/ppermute | solution.py:384
  169.3 8.6 %collective-permute-start.9 = (f32[512,256]{1,0:T(8,128)S(1)}, f32[512,256]{1,0:T(8,128)S(1)}, u32[]{:S(2)}, u32[]{:S(2)}) collective-permute-start(f32[512,256]{1,0:T(8,128)S(1)} %get-tuple-element.80), channel_id=1, source_target_pairs={{0,112},{16,0},{32,16},{48,32},{64,48},{80,64},{96,80},{112,96},{1... | collective-permute-start | bytes 1572872 | tf_op jit(solution)/shard_map/ppermute | solution.py:384
where the time goes:
time: 180 us
  blocking collectives  98.7 us (55%)
  Pallas kernels  53.2 us (30%)
  starting transfers between devices  14.9 us (8%)
  waiting for transfers between devices  11 us (6%)
    all_to_all x3, blocking collectives, sum_rows(): pieces = lax.all_to_all(part, 'row', 0, 0, tiled=True)  52 us
    all_to_all x3, blocking collectives, sum_rows(): return lax.all_to_all(mine, 'row', 0, 0, tiled=True)  46.6 us
    pallas_call x3, Pallas kernels, body(): call(partial(kernel, total_rows, slots), (block, block) + (bf16((pairs,)...  31 us
    ppermute x10, starting transfers between devices, to_next(): lax.ppermute(x, 'pair', [(i, (i + by) % count) for i in range(count)])  14.9 us
    ppermute x10, waiting for transfers between devices, to_next(): lax.ppermute(x, 'pair', [(i, (i + by) % count) for i in range(count)])  11 us
    pallas_call x2, Pallas kernels, body(): call(partial(carry_self, index, slots), (f32((slots, BLOCK, BLOCK)), smal...  7.05 us
    pallas_call x2, Pallas kernels, body(): call(partial(apply, slots), f32((slots, rows, BLOCK)), [VMEM] * 4 + [ANY]...  3.9 us
  transfers between devices with their start and end apart: 10, of which 6 were waited for; matrix products, arithmetic and copies ran while one was open for 0% of the time, Pallas kernels for 10%

commit v1 on v0

--- a/solution.py
+++ b/solution.py
@@ -9,6 +9,7 @@
 
 BLOCK = 256
 PAIR = 2 * BLOCK
+LANES = 128
 ROUNDS = 3
 UNROLLED = (0, 1, 2)
 F32 = jnp.float32
@@ -81,10 +82,9 @@
 
 def first_gram(a_ref, part_ref, high_ref, low_ref):
     pairs = a_ref.shape[1] // PAIR
-    chunks = part_ref.shape[0]
-    rows = part_ref.shape[1] - 8
+    rows = (part_ref.shape[1] - 8) // 2
     per = BLOCK // rows
-    part_ref[:, rows:, :] = jnp.zeros((chunks, 8, BLOCK), F32)
+    part_ref[:, 2 * rows:, :] = jnp.zeros((part_ref.shape[0], 8, LANES), F32)
     for p in range(pairs):
         one, two = pl.ds(p * PAIR, BLOCK), pl.ds(p * PAIR + BLOCK, BLOCK)
         for cols in (one, two):
@@ -102,10 +102,13 @@
         diagonal = jnp.sum(jnp.where(eye, second, 0.0), axis=0, keepdims=True)
         both = jnp.where(eye | upper_mask(BLOCK), first, second)
         start = 2 * per * p
-        for j in range(per):
-            part_ref[start + j, :rows, :] = cross[j * rows:(j + 1) * rows]
-            part_ref[start + per + j, :rows, :] = both[j * rows:(j + 1) * rows]
-        part_ref[start, rows:, :] = jnp.broadcast_to(diagonal, (8, BLOCK))
+        for first_chunk, block in ((start, cross), (start + per, both)):
+            for j in range(per):
+                piece = block[j * rows:(j + 1) * rows]
+                part_ref[first_chunk + j, :rows, :] = piece[:, :LANES]
+                part_ref[first_chunk + j, rows:2 * rows, :] = piece[:, LANES:]
+        part_ref[start, 2 * rows:2 * rows + 1, :] = diagonal[:, :LANES]
+        part_ref[start, 2 * rows + 1:2 * rows + 2, :] = diagonal[:, LANES:]
 
 
 def cross_gram(round_index, slots, src_ref, dev_ref, own_ref, lower_ref, upper_ref, part_ref, high_ref, low_ref):
@@ -266,16 +269,20 @@
 
 def first_rotate(total_rows, slots, src_ref, dev_ref, sum_ref, high_ref, low_ref,
                  right_ref, left_ref, rh_ref, rl_ref, gh_ref, gl_ref, *rest):
-    rows = sum_ref.shape[1] - 8
+    rows = (sum_ref.shape[1] - 8) // 2
     per = BLOCK // rows
     works = [rest[at:at + 15] for at in range(0, len(rest), 15)]
     lo, hi = pl.ds(0, BLOCK), pl.ds(BLOCK, BLOCK)
 
     def generator(p, work):
         first_chunk = 2 * per * p
-        cross = sum_ref[pl.ds(first_chunk, per), :rows, :].reshape(BLOCK, BLOCK)
-        both = sum_ref[pl.ds(first_chunk + per, per), :rows, :].reshape(BLOCK, BLOCK)
-        diagonal = sum_ref[first_chunk, rows:rows + 1, :]
+
+        def unpack(chunk):
+            halves = [sum_ref[pl.ds(chunk, per), pl.ds(at, rows), :].reshape(BLOCK, LANES) for at in (0, rows)]
+            return jnp.concatenate(halves, axis=1)
+
+        cross, both = unpack(first_chunk), unpack(first_chunk + per)
+        diagonal = jnp.concatenate([sum_ref[first_chunk, pl.ds(2 * rows + at, 1), :] for at in (0, 1)], axis=1)
         turned = both.T
         eye, upper = eye_mask(BLOCK), upper_mask(BLOCK)
         first = jnp.where(eye | upper, both, turned)
@@ -333,12 +340,6 @@
     left_ref[...] = self_ref[leaving(src_ref, dev_ref, round_index, -1, slots)]
 
 
-def take_self(round_index, slots, src_ref, dev_ref, self_ref, lower_ref, upper_ref, after_ref, out_ref):
-    for slot in range(slots):
-        offset = own_source(src_ref, dev_ref, round_index, slot, slots)
-        out_ref[slot] = picked(offset, slots, self_ref, lower_ref, upper_ref)
-
-
 def apply(slots, high_ref, low_ref, rh_ref, rl_ref, after_ref, own_ref):
     @pl.loop(0, slots // 2)
     def _(p):
@@ -390,10 +391,15 @@
         out_ref[chunk] = total
 
 
-def sum_rows(part):
-    pieces = lax.all_to_all(part, "row", 0, 0, tiled=True)
-    mine = call(add_up, jax.ShapeDtypeStruct(part.shape, F32), [VMEM])(pieces)
-    return lax.all_to_all(mine, "row", 0, 0, tiled=True)
+def add_up_and_take(round_index, slots, src_ref, dev_ref, pieces_ref, self_ref, lower_ref, upper_ref, out_ref, taken_ref):
+    add_up(pieces_ref, out_ref)
+    for slot in range(slots):
+        offset = own_source(src_ref, dev_ref, round_index, slot, slots)
+        taken_ref[slot] = picked(offset, slots, self_ref, lower_ref, upper_ref)
+
+
+def from_rows(part):
+    return lax.all_to_all(part, "row", 0, 0, tiled=True)
 
 
 def body(matrix, sources):
@@ -412,16 +418,16 @@
     sems = pltpu.SemaphoreType.DMA((slots,))
     part, high, low = call(
         first_gram,
-        (f32((row_count, 2 * slots * BLOCK // 2 // row_count + 8, BLOCK)), bf16(matrix.shape), bf16(matrix.shape)),
+        (f32((row_count, BLOCK // LANES * slots * BLOCK // row_count + 8, LANES)), bf16(matrix.shape), bf16(matrix.shape)),
         [VMEM],
         flops=3 * pairs * product_flops // 4,
     )(matrix)
     part, sources, device = lax.optimization_barrier((part, sources, device))
     block, small = f32((rows, BLOCK)), f32((BLOCK, BLOCK))
     carried = ()
+    summed = from_rows(call(add_up, f32(part.shape), [VMEM])(from_rows(part)))
     for index in range(ROUNDS):
         last = index == ROUNDS - 1
-        summed = sum_rows(part)
         kernel = first_rotate if index == 0 else partial(later_rotate, index, last)
         right, left, rh, rl, *gram = call(
             partial(kernel, total_rows, slots),
@@ -469,10 +475,14 @@
             [SMEM, SMEM] + [VMEM] * 3,
             flops=pairs * product_flops // 4,
         )(sources, device, own, lower, upper)
-        selves = call(
-            partial(take_self, index, slots), f32((slots, BLOCK, BLOCK)), [SMEM, SMEM] + [VMEM] * 3 + [ANY]
-        )(sources, device, selves, lower_self, upper_self, part)
-        part, *carried = lax.optimization_barrier((part, selves))
+        part, lower_self, upper_self = lax.optimization_barrier((part, lower_self, upper_self))
+        mine, selves = call(
+            partial(add_up_and_take, index, slots),
+            (f32(part.shape), f32((slots, BLOCK, BLOCK))),
+            [SMEM, SMEM] + [VMEM] * 4,
+        )(sources, device, from_rows(part), selves, lower_self, upper_self)
+        carried = (selves,)
+        summed = from_rows(mine)
 
 
 def solution(mesh):

time: 180 us -> 179 us (level)
  no operation moved by 1% of the time
where the time goes in v1:
time: 179 us; the launch traced here: 178 us
  blocking collectives  97.4 us (54%)
  Pallas kernels  53.2 us (30%)
  starting transfers between devices  15 us (8%)
  waiting for transfers between devices  11 us (6%)
    all_to_all x6, blocking collectives, from_rows(): return lax.all_to_all(part, 'row', 0, 0, tiled=True)  97.4 us
    pallas_call x3, Pallas kernels, body(): call(partial(kernel, total_rows, slots), (block, block) + (bf16((pairs,)...  31 us
    ppermute x10, starting transfers between devices, to_next(): lax.ppermute(x, 'pair', [(i, (i + by) % count) for i in range(count)])  15 us
    ppermute x10, waiting for transfers between devices, to_next(): lax.ppermute(x, 'pair', [(i, (i + by) % count) for i in range(count)])  11 us
    pallas_call x2, Pallas kernels, body(): call(partial(carry_self, index, slots), (f32((slots, BLOCK, BLOCK)), smal...  7.05 us
    pallas_call x2, Pallas kernels, body(): call(partial(apply, slots), f32((slots, rows, BLOCK)), [VMEM] * 4 + [ANY]...  3.9 us
  transfers between devices with their start and end apart: 10, of which 6 were waited for; matrix products, arithmetic and copies ran while one was open for 0% of the time, Pallas kernels for 10%

profile of v1, /device:TPU:1, one launch (start us, length us, event | category | flops | bytes accessed | tf_op | source)
XLA Modules:
  0.0 178.4 jit_solution(13917699858305258267)
XLA Ops:
  0.0 1.6 copy-done.1
  3.1 25.1 %all_to_all.30.pieces_ref = f32[16,136,128]{2,1,0:T(8,128)S(1)} all-to-all(f32[16,136,128]{2,1,0:T(8,128)S(1)} %get-tuple-element.54), channel_id=1, replica_groups=mesh['pair'=8,'row'=16] {'row'}, dimensions={0} | all-to-all | bytes 2228224 | tf_op jit(solution)/shard_map/all_to_all | solution.py:402
  28.3 19.0 %all_to_all.31.sum_ref = f32[16,136,128]{2,1,0:T(8,128)S(1)} all-to-all(f32[16,136,128]{2,1,0:T(8,128)S(1)} %shard_map.29), channel_id=1, replica_groups=mesh['pair'=8,'row'=16] {'row'}, dimensions={0} | all-to-all | bytes 2228224 | tf_op jit(solution)/shard_map/all_to_all | solution.py:402
  47.3 10.4 %shard_map.30 = (f32[512,256]{1,0:T(8,128)S(1)}, f32[512,256]{1,0:T(8,128)S(1)}, bf16[2,512,512]{2,1,0:T(8,128)(2,1)S(1)}, bf16[2,512,512]{2,1,0:T(8,128)(2,1)S(...) custom-call(s32[3,32]{1,0:T(4,128)S(1)} %copy-done, s32[1]{0:T(128)} %bitcast.dev_ref, ...), custom_call_target="tpu_custom_call" | custom-call | flops 11274289152 | bytes 4000000 | tf_op jit(solution)/shard_map/pallas_call | solution.py:432
  57.8 4.3 %collective-permute-start = (f32[512,256]{1,0:T(8,128)S(1)}, f32[512,256]{1,0:T(8,128)S(1)}, u32[]{:S(2)}, u32[]{:S(2)}) collective-permute-start(f32[512,256]{1,0:T(8,128)S(1)} %get-tuple-element.60), channel_id=1, source_target_pairs={{0,16},{16,32},{32,48},{48,64},{64,80},{80,96},{96,112},{112,0},{1... | collective-permute-start | bytes 1572872 | tf_op jit(solution)/shard_map/ppermute | solution.py:385
  62.0 3.5 %shard_map.31 = (f32[4,256,256]{2,1,0:T(8,128)S(1)}, f32[256,256]{1,0:T(8,128)S(1)}, f32[256,256]{1,0:T(8,128)S(1)}) custom-call(s32[3,32]{1,0:T(4,128)S(1)} %copy-done, s32[1]{0:T(128)} %bitcast.dev_ref, bf16[2,512,512]{2,1,0:T(8,128)(2,1)S(1)} %get-tuple-element.57.gh_ref, bf16[2,512,512]{2,1,0:T(8,128)(2,1)S(1)} %get-tuple-element.58.gl_ref, ...), custom_call_target="tpu_custom_call" | custom-call | flops 2415919104 | bytes 4000000 | tf_op jit(solution)/shard_map/pallas_call | solution.py:458
  65.6 1.8 collective-permute-start.2
  67.4 1.9 %shard_map.32.own_ref = f32[4,512,256]{2,1,0:T(8,128)S(1)} custom-call(bf16[512,1024]{1,0:T(8,128)(2,1)S(1)} %get-tuple-element.52.high_ref, bf16[512,1024]{1,0:T(8,128)(2,1)S(1)} %get-tuple-element.53.low_ref, bf16[2,512,512]{2,1,0:T(8,128)(2,1)S(1)} %get-tuple-element.55.rh_ref, bf16[2,512,512]{2,1,0:T(8,128)(2,1)S(1)} %get-tuple-element.56.rl_ref, ...), custom_call_target="tpu_custom_call" | custom-call | flops 1610612736 | bytes 4000000 | tf_op jit(solution)/shard_map/pallas_call | solution.py:465
  72.1 1.6 collective-permute-done.3.upper_ref
  73.8 13.2 %all_to_all.32.pieces_ref = f32[16,32,256]{2,1,0:T(8,128)S(1)} all-to-all(f32[16,32,256]{2,1,0:T(8,128)S(1)} %get-tuple-element.67), channel_id=1, replica_groups=mesh['pair'=8,'row'=16] {'row'}, dimensions={0} | all-to-all | bytes 1048576 | tf_op jit(solution)/shard_map/all_to_all | solution.py:402
  87.8 13.4 %all_to_all.33.sum_ref = f32[16,32,256]{2,1,0:T(8,128)S(1)} all-to-all(f32[16,32,256]{2,1,0:T(8,128)S(1)} %get-tuple-element.70), channel_id=1, replica_groups=mesh['pair'=8,'row'=16] {'row'}, dimensions={0} | all-to-all | bytes 1048576 | tf_op jit(solution)/shard_map/all_to_all | solution.py:402
  101.2 10.3 %shard_map.35 = (f32[512,256]{1,0:T(8,128)S(1)}, f32[512,256]{1,0:T(8,128)S(1)}, bf16[2,512,512]{2,1,0:T(8,128)(2,1)S(1)}, bf16[2,512,512]{2,1,0:T(8,128)(2,1)S(...) custom-call(s32[3,32]{1,0:T(4,128)S(1)} %copy-done, s32[1]{0:T(128)} %bitcast.dev_ref, ...), custom_call_target="tpu_custom_call" | custom-call | flops 11274289152 | bytes 4000000 | tf_op jit(solution)/shard_map/pallas_call | solution.py:432
  111.5 3.7 %collective-permute-start.4 = (f32[512,256]{1,0:T(8,128)S(1)}, f32[512,256]{1,0:T(8,128)S(1)}, u32[]{:S(2)}, u32[]{:S(2)}) collective-permute-start(f32[512,256]{1,0:T(8,128)S(1)} %get-tuple-element.77), channel_id=1, source_target_pairs={{0,16},{16,32},{32,48},{48,64},{64,80},{80,96},{96,112},{112,0},{1... | collective-permute-start | bytes 1572872 | tf_op jit(solution)/shard_map/ppermute | solution.py:385
  115.2 3.5 %shard_map.36 = (f32[4,256,256]{2,1,0:T(8,128)S(1)}, f32[256,256]{1,0:T(8,128)S(1)}, f32[256,256]{1,0:T(8,128)S(1)}) custom-call(s32[3,32]{1,0:T(4,128)S(1)} %copy-done, s32[1]{0:T(128)} %bitcast.dev_ref, bf16[2,512,512]{2,1,0:T(8,128)(2,1)S(1)} %get-tuple-element.74.gh_ref, bf16[2,512,512]{2,1,0:T(8,128)(2,1)S(1)} %get-tuple-element.75.gl_ref, ...), custom_call_target="tpu_custom_call" | custom-call | flops 2415919104 | bytes 4000000 | tf_op jit(solution)/shard_map/pallas_call | solution.py:458
  118.8 1.8 collective-permute-start.6
  120.5 1.9 %shard_map.37.own_ref = f32[4,512,256]{2,1,0:T(8,128)S(1)} custom-call(bf16[512,1024]{1,0:T(8,128)(2,1)S(1)} %get-tuple-element.62.high_ref, bf16[512,1024]{1,0:T(8,128)(2,1)S(1)} %get-tuple-element.63.low_ref, bf16[2,512,512]{2,1,0:T(8,128)(2,1)S(1)} %get-tuple-element.72.rh_ref, bf16[2,512,512]{2,1,0:T(8,128)(2,1)S(1)} %get-tuple-element.73.rl_ref, ...), custom_call_target="tpu_custom_call" | custom-call | flops 1610612736 | bytes 4000000 | tf_op jit(solution)/shard_map/pallas_call | solution.py:465
  125.3 1.6 collective-permute-done.7.upper_ref
  126.9 13.2 %all_to_all.34.pieces_ref = f32[16,32,256]{2,1,0:T(8,128)S(1)} all-to-all(f32[16,32,256]{2,1,0:T(8,128)S(1)} %get-tuple-element.84), channel_id=1, replica_groups=mesh['pair'=8,'row'=16] {'row'}, dimensions={0} | all-to-all | bytes 1048576 | tf_op jit(solution)/shard_map/all_to_all | solution.py:402
  140.9 13.4 %all_to_all.35.sum_ref = f32[16,32,256]{2,1,0:T(8,128)S(1)} all-to-all(f32[16,32,256]{2,1,0:T(8,128)S(1)} %get-tuple-element.87), channel_id=1, replica_groups=mesh['pair'=8,'row'=16] {'row'}, dimensions={0} | all-to-all | bytes 1048576 | tf_op jit(solution)/shard_map/all_to_all | solution.py:402
  154.4 10.2 %shard_map.40 = (f32[512,256]{1,0:T(8,128)S(1)}, f32[512,256]{1,0:T(8,128)S(1)}, bf16[2,512,512]{2,1,0:T(8,128)(2,1)S(1)}, bf16[2,512,512]{2,1,0:T(8,128)(2,1)S(1)}) custom-call(s32[3,32]{1,0:T(4,128)S(1)} %copy-done, s32[1]{0:T(128)} %bitcast.dev_ref, f32[16,32,256]{2,1,0:T(8,128)S(1)} %all_to_all.35.sum_ref, ...), custom_call_target="tpu_custom_call" | custom-call | flops 11274289152 | bytes 4000000 | tf_op jit(solution)/shard_map/pallas_call | solution.py:432
  164.6 3.4 %collective-permute-start.8 = (f32[512,256]{1,0:T(8,128)S(1)}, f32[512,256]{1,0:T(8,128)S(1)}, u32[]{:S(2)}, u32[]{:S(2)}) collective-permute-start(f32[512,256]{1,0:T(8,128)S(1)} %get-tuple-element.91), channel_id=1, source_target_pairs={{0,16},{16,32},{32,48},{48,64},{64,80},{80,96},{96,112},{112,0},{1... | collective-permute-start | bytes 1572872 | tf_op jit(solution)/shard_map/ppermute | solution.py:385
  168.1 3.5 %shard_map.41.most_ref = f32[512,1024]{1,0:T(8,128)} custom-call(s32[3,32]{1,0:T(4,128)S(1)} %copy-done, s32[1]{0:T(128)} %bitcast.dev_ref, bf16[512,1024]{1,0:T(8,128)(2,1)S(1)} %get-tuple-element.79.high_ref, bf16[512,1024]{1,0:T(8,128)(2,1)S(1)} %get-tuple-element.80.low_ref, bf16[2,512,512]{2,1,0:T(8,128)(2,1)S(1)} %get-tuple-element.89.rh_ref, ...), custom_call_target="tpu_custom_call" | custom-call | flops 1610612736 | bytes 4000000 | tf_op jit(solution)/shard_map/pallas_call | solution.py:442
  171.6 2.6 %collective-permute-done.8.lower_ref = f32[512,256]{1,0:T(8,128)S(1)} collective-permute-done((f32[512,256]{1,0:T(8,128)S(1)}, f32[512,256]{1,0:T(8,128)S(1)}, u32[]{:S(2)}, u32[]{:S(2)}) %collective-permute-start.8) | collective-permute-done | bytes 524320 | tf_op jit(solution)/shard_map/ppermute | solution.py:385
  174.2 2.5 %collective-permute-done.9.upper_ref = f32[512,256]{1,0:T(8,128)S(1)} collective-permute-done((f32[512,256]{1,0:T(8,128)S(1)}, f32[512,256]{1,0:T(8,128)S(1)}, u32[]{:S(2)}, u32[]{:S(2)}) %collective-permute-start.9) | collective-permute-done | bytes 524320 | tf_op jit(solution)/shard_map/ppermute | solution.py:385
  (21 shorter events, 10.4 us)
Async XLA Ops:
  0.0 1.6 copy-start.1
  28.2 19.1 %copy-start = (s32[3,32]{1,0:T(4,128)S(1)}, s32[3,32]{1,0:T(4,128)}, u32[]{:S(2)}) copy-start(s32[3,32]{1,0:T(4,128)} %src_ref.10) | copy-start | bytes 1156
  57.8 11.6 %collective-permute-start = (f32[512,256]{1,0:T(8,128)S(1)}, f32[512,256]{1,0:T(8,128)S(1)}, u32[]{:S(2)}, u32[]{:S(2)}) collective-permute-start(f32[512,256]{1,0:T(8,128)S(1)} %get-tuple-element.60), channel_id=1, source_target_pairs={{0,16},{16,32},{32,48},{48,64},{64,80},{80,96},{96,112},{112,0},{1... | collective-permute-start | bytes 1572872 | tf_op jit(solution)/shard_map/ppermute | solution.py:385
  62.0 8.6 %collective-permute-start.1 = (f32[512,256]{1,0:T(8,128)S(1)}, f32[512,256]{1,0:T(8,128)S(1)}, u32[]{:S(2)}, u32[]{:S(2)}) collective-permute-start(f32[512,256]{1,0:T(8,128)S(1)} %get-tuple-element.61), channel_id=1, source_target_pairs={{0,112},{16,0},{32,16},{48,32},{64,48},{80,64},{96,80},{112,96},{1... | collective-permute-start | bytes 1572872 | tf_op jit(solution)/shard_map/ppermute | solution.py:385
  65.6 6.6 %collective-permute-start.2 = (f32[256,256]{1,0:T(8,128)S(1)}, f32[256,256]{1,0:T(8,128)S(1)}, u32[]{:S(2)}, u32[]{:S(2)}) collective-permute-start(f32[256,256]{1,0:T(8,128)S(1)} %get-tuple-element.65), channel_id=1, source_target_pairs={{0,16},{16,32},{32,48},{48,64},{64,80},{80,96},{96,112},{112,0},{1... | collective-permute-start | bytes 786440 | tf_op jit(solution)/shard_map/ppermute | solution.py:385
  67.3 6.4 %collective-permute-start.3 = (f32[256,256]{1,0:T(8,128)S(1)}, f32[256,256]{1,0:T(8,128)S(1)}, u32[]{:S(2)}, u32[]{:S(2)}) collective-permute-start(f32[256,256]{1,0:T(8,128)S(1)} %get-tuple-element.66), channel_id=1, source_target_pairs={{0,112},{16,0},{32,16},{48,32},{64,48},{80,64},{96,80},{112,96},{1... | collective-permute-start | bytes 786440 | tf_op jit(solution)/shard_map/ppermute | solution.py:385
  111.5 10.9 %collective-permute-start.4 = (f32[512,256]{1,0:T(8,128)S(1)}, f32[512,256]{1,0:T(8,128)S(1)}, u32[]{:S(2)}, u32[]{:S(2)}) collective-permute-start(f32[512,256]{1,0:T(8,128)S(1)} %get-tuple-element.77), channel_id=1, source_target_pairs={{0,16},{16,32},{32,48},{48,64},{64,80},{80,96},{96,112},{112,0},{1... | collective-permute-start | bytes 1572872 | tf_op jit(solution)/shard_map/ppermute | solution.py:385
  115.2 8.6 %collective-permute-start.5 = (f32[512,256]{1,0:T(8,128)S(1)}, f32[512,256]{1,0:T(8,128)S(1)}, u32[]{:S(2)}, u32[]{:S(2)}) collective-permute-start(f32[512,256]{1,0:T(8,128)S(1)} %get-tuple-element.78), channel_id=1, source_target_pairs={{0,112},{16,0},{32,16},{48,32},{64,48},{80,64},{96,80},{112,96},{1... | collective-permute-start | bytes 1572872 | tf_op jit(solution)/shard_map/ppermute | solution.py:385
  118.8 6.6 %collective-permute-start.6 = (f32[256,256]{1,0:T(8,128)S(1)}, f32[256,256]{1,0:T(8,128)S(1)}, u32[]{:S(2)}, u32[]{:S(2)}) collective-permute-start(f32[256,256]{1,0:T(8,128)S(1)} %get-tuple-element.82), channel_id=1, source_target_pairs={{0,16},{16,32},{32,48},{48,64},{64,80},{80,96},{96,112},{112,0},{1... | collective-permute-start | bytes 786440 | tf_op jit(solution)/shard_map/ppermute | solution.py:385
  120.5 6.4 %collective-permute-start.7 = (f32[256,256]{1,0:T(8,128)S(1)}, f32[256,256]{1,0:T(8,128)S(1)}, u32[]{:S(2)}, u32[]{:S(2)}) collective-permute-start(f32[256,256]{1,0:T(8,128)S(1)} %get-tuple-element.83), channel_id=1, source_target_pairs={{0,112},{16,0},{32,16},{48,32},{64,48},{80,64},{96,80},{112,96},{1... | collective-permute-start | bytes 786440 | tf_op jit(solution)/shard_map/ppermute | solution.py:385
  164.6 9.6 %collective-permute-start.8 = (f32[512,256]{1,0:T(8,128)S(1)}, f32[512,256]{1,0:T(8,128)S(1)}, u32[]{:S(2)}, u32[]{:S(2)}) collective-permute-start(f32[512,256]{1,0:T(8,128)S(1)} %get-tuple-element.91), channel_id=1, source_target_pairs={{0,16},{16,32},{32,48},{48,64},{64,80},{80,96},{96,112},{112,0},{1... | collective-permute-start | bytes 1572872 | tf_op jit(solution)/shard_map/ppermute | solution.py:385
  168.1 8.6 %collective-permute-start.9 = (f32[512,256]{1,0:T(8,128)S(1)}, f32[512,256]{1,0:T(8,128)S(1)}, u32[]{:S(2)}, u32[]{:S(2)}) collective-permute-start(f32[512,256]{1,0:T(8,128)S(1)} %get-tuple-element.92), channel_id=1, source_target_pairs={{0,112},{16,0},{32,16},{48,32},{64,48},{80,64},{96,80},{112,96},{1... | collective-permute-start | bytes 1572872 | tf_op jit(solution)/shard_map/ppermute | solution.py:385

commit v2 on v1

--- a/solution.py
+++ b/solution.py
@@ -59,13 +59,13 @@
     return lax.broadcasted_iota(jnp.int32, (n, n), 0) < lax.broadcasted_iota(jnp.int32, (n, n), 1)
 
 
-def own_source(src_ref, dev_ref, round_index, slot, slots):
-    base = dev_ref[0] * slots
+def own_source(src_ref, round_index, slot, slots):
+    base = lax.axis_index("pair") * slots
     return src_ref[round_index, base + slot] - base
 
 
-def leaving(src_ref, dev_ref, round_index, step, slots):
-    base = dev_ref[0] * slots
+def leaving(src_ref, round_index, step, slots):
+    base = lax.axis_index("pair") * slots
     last = src_ref.shape[1] - slots
     there = jnp.clip(base + step * slots, 0, last)
     found = jnp.int32(0)
@@ -111,11 +111,11 @@
         part_ref[start, 2 * rows + 1:2 * rows + 2, :] = diagonal[:, LANES:]
 
 
-def cross_gram(round_index, slots, src_ref, dev_ref, own_ref, lower_ref, upper_ref, part_ref, high_ref, low_ref):
+def cross_gram(round_index, slots, src_ref, own_ref, lower_ref, upper_ref, part_ref, high_ref, low_ref):
     rows = part_ref.shape[1]
     per = BLOCK // rows
     for slot in range(slots):
-        offset = own_source(src_ref, dev_ref, round_index, slot, slots)
+        offset = own_source(src_ref, round_index, slot, slots)
         high, low = split(picked(offset, slots, own_ref, lower_ref, upper_ref))
         high_ref[:, pl.ds(slot * BLOCK, BLOCK)] = high
         low_ref[:, pl.ds(slot * BLOCK, BLOCK)] = low
@@ -256,9 +256,15 @@
                 stage(p)
 
 
-def leave(round_index, slots, src_ref, dev_ref, high_ref, low_ref, rh_ref, rl_ref, right_ref, left_ref):
+def fetch(table_ref, held, sem):
+    copy = pltpu.make_async_copy(table_ref, held, sem)
+    copy.start()
+    return copy
+
+
+def leave(round_index, slots, src_ref, high_ref, low_ref, rh_ref, rl_ref, right_ref, left_ref):
     for step, out_ref in ((1, right_ref), (-1, left_ref)):
-        slot = leaving(src_ref, dev_ref, round_index, step, slots)
+        slot = leaving(src_ref, round_index, step, slots)
         pair, half = slot >> 1, slot & 1
         rows = pl.ds(pl.multiple_of(pair * PAIR, PAIR), PAIR)
         cols = pl.ds(pl.multiple_of(half * BLOCK, BLOCK), BLOCK)
@@ -267,8 +273,9 @@
         )
 
 
-def first_rotate(total_rows, slots, src_ref, dev_ref, sum_ref, high_ref, low_ref,
-                 right_ref, left_ref, rh_ref, rl_ref, gh_ref, gl_ref, *rest):
+def first_rotate(total_rows, slots, table_ref, sum_ref, high_ref, low_ref,
+                 right_ref, left_ref, rh_ref, rl_ref, gh_ref, gl_ref, src_ref, sem, *rest):
+    table = fetch(table_ref, src_ref, sem)
     rows = (sum_ref.shape[1] - 8) // 2
     per = BLOCK // rows
     works = [rest[at:at + 15] for at in range(0, len(rest), 15)]
@@ -294,16 +301,18 @@
         return set_generator(total_rows, cross, first, second, *work[:3])
 
     rotations(slots // 2, generator, works, rh_ref, rl_ref)
-    leave(0, slots, src_ref, dev_ref, high_ref, low_ref, rh_ref, rl_ref, right_ref, left_ref)
-
-
-def later_rotate(round_index, last, total_rows, slots, src_ref, dev_ref, sum_ref, self_ref,
+    table.wait()
+    leave(0, slots, src_ref, high_ref, low_ref, rh_ref, rl_ref, right_ref, left_ref)
+
+
+def later_rotate(round_index, last, total_rows, slots, table_ref, sum_ref, self_ref,
                  high_ref, low_ref, right_ref, left_ref, rh_ref, rl_ref, *rest):
     rows = sum_ref.shape[1]
     per = BLOCK // rows
     if not last:
         gh_ref, gl_ref = rest[:2]
-    rest = rest if last else rest[2:]
+    src_ref, sem, *rest = rest if last else rest[2:]
+    table = fetch(table_ref, src_ref, sem)
     works = [rest[at:at + 15] for at in range(0, len(rest), 15)]
     lo, hi = pl.ds(0, BLOCK), pl.ds(BLOCK, BLOCK)
 
@@ -318,11 +327,13 @@
         return set_generator(total_rows, cross, first, second, *work[:3])
 
     rotations(slots // 2, generator, works, rh_ref, rl_ref)
-    leave(round_index, slots, src_ref, dev_ref, high_ref, low_ref, rh_ref, rl_ref, right_ref, left_ref)
-
-
-def carry_self(round_index, slots, src_ref, dev_ref, gh_ref, gl_ref, rh_ref, rl_ref,
-               self_ref, right_ref, left_ref, *work):
+    table.wait()
+    leave(round_index, slots, src_ref, high_ref, low_ref, rh_ref, rl_ref, right_ref, left_ref)
+
+
+def carry_self(round_index, slots, table_ref, gh_ref, gl_ref, rh_ref, rl_ref,
+               self_ref, right_ref, left_ref, src_ref, sem, *work):
+    table = fetch(table_ref, src_ref, sem)
     @pl.loop(0, slots // 2)
     def _(p):
         for half in range(2):
@@ -336,8 +347,13 @@
                 dot_t(rh_ref[p, :, cols], yl[...]) + dot_t(rl_ref[p, :, cols], yh[...])
             )
 
-    right_ref[...] = self_ref[leaving(src_ref, dev_ref, round_index, 1, slots)]
-    left_ref[...] = self_ref[leaving(src_ref, dev_ref, round_index, -1, slots)]
+    table.wait()
+    for step, out_ref in ((1, right_ref), (-1, left_ref)):
+        slot = leaving(src_ref, round_index, step, slots)
+        out_ref[:LANES, :] = self_ref[slot, :LANES, :]
+        for half in range(2):
+            rows = pl.ds(LANES + half * LANES // 2, LANES // 2)
+            out_ref[LANES:, pl.ds(half * LANES, LANES)] = self_ref[slot, rows, LANES:]
 
 
 def apply(slots, high_ref, low_ref, rh_ref, rl_ref, after_ref, own_ref):
@@ -350,9 +366,11 @@
             )
 
 
-def apply_last(round_index, slots, src_ref, dev_ref, high_ref, low_ref, rh_ref, rl_ref, out_ref, own_ref, sems):
+def apply_last(round_index, slots, table_ref, high_ref, low_ref, rh_ref, rl_ref, out_ref, src_ref, sem, own_ref, sems):
+    table = fetch(table_ref, src_ref, sem)
     apply(slots, high_ref, low_ref, rh_ref, rl_ref, None, own_ref)
-    offsets = [own_source(src_ref, dev_ref, round_index, slot, slots) for slot in range(slots)]
+    table.wait()
+    offsets = [own_source(src_ref, round_index, slot, slots) for slot in range(slots)]
     for wait in (False, True):
         for slot, offset in enumerate(offsets):
             @pl.when((offset >= 0) & (offset < slots))
@@ -363,8 +381,8 @@
                 copy.wait() if wait else copy.start()
 
 
-def settle(round_index, slots, src_ref, dev_ref, most_ref, lower_ref, upper_ref, out_ref, sems):
-    offsets = [own_source(src_ref, dev_ref, round_index, slot, slots) for slot in range(slots)]
+def settle(round_index, slots, src_ref, most_ref, lower_ref, upper_ref, out_ref, sems):
+    offsets = [own_source(src_ref, round_index, slot, slots) for slot in range(slots)]
     for wait in (False, True):
         for slot, offset in enumerate(offsets):
             goal = out_ref.at[:, pl.ds(slot * BLOCK, BLOCK)]
@@ -391,11 +409,20 @@
         out_ref[chunk] = total
 
 
-def add_up_and_take(round_index, slots, src_ref, dev_ref, pieces_ref, self_ref, lower_ref, upper_ref, out_ref, taken_ref):
+def add_up_and_take(round_index, slots, table_ref, pieces_ref, self_ref, lower_ref, upper_ref,
+                    out_ref, taken_ref, src_ref, sem, lower_full, upper_full):
+    table = fetch(table_ref, src_ref, sem)
     add_up(pieces_ref, out_ref)
+    for packed, full in ((lower_ref, lower_full), (upper_ref, upper_full)):
+        full[:LANES, :] = packed[:LANES, :]
+        full[LANES:, :LANES] = packed[:LANES, LANES:].T
+        for half in range(2):
+            rows = pl.ds(LANES + half * LANES // 2, LANES // 2)
+            full[rows, LANES:] = packed[LANES:, pl.ds(half * LANES, LANES)]
+    table.wait()
     for slot in range(slots):
-        offset = own_source(src_ref, dev_ref, round_index, slot, slots)
-        taken_ref[slot] = picked(offset, slots, self_ref, lower_ref, upper_ref)
+        offset = own_source(src_ref, round_index, slot, slots)
+        taken_ref[slot] = picked(offset, slots, self_ref, lower_full, upper_full)
 
 
 def from_rows(part):
@@ -408,7 +435,6 @@
     pairs = slots // 2
     row_count = lax.axis_size("row")
     total_rows = rows * row_count
-    device = lax.axis_index("pair").astype(jnp.int32).reshape(1)
     f32 = partial(jax.ShapeDtypeStruct, dtype=F32)
     bf16 = partial(jax.ShapeDtypeStruct, dtype=BF16)
     square = (PAIR, PAIR)
@@ -422,8 +448,9 @@
         [VMEM],
         flops=3 * pairs * product_flops // 4,
     )(matrix)
-    part, sources, device = lax.optimization_barrier((part, sources, device))
-    block, small = f32((rows, BLOCK)), f32((BLOCK, BLOCK))
+    part, sources = lax.optimization_barrier((part, sources))
+    block, small = f32((rows, BLOCK)), f32((BLOCK * 3 // 4, BLOCK))
+    table = [pltpu.SMEM(sources.shape, jnp.int32), pltpu.SemaphoreType.DMA]
     carried = ()
     summed = from_rows(call(add_up, f32(part.shape), [VMEM])(from_rows(part)))
     for index in range(ROUNDS):
@@ -432,36 +459,36 @@
         right, left, rh, rl, *gram = call(
             partial(kernel, total_rows, slots),
             (block, block) + (bf16((pairs,) + square),) * (2 if last else 4),
-            [SMEM, SMEM] + [VMEM] * (3 + len(carried)),
-            work * (pairs if index in UNROLLED else 1),
+            [ANY] + [VMEM] * (3 + len(carried)),
+            table + work * (pairs if index in UNROLLED else 1),
             flops=7 * pairs * product_flops,
             mib=20,
-        )(sources, device, summed, *carried, high, low)
+        )(sources, summed, *carried, high, low)
         lower, upper = to_next(right, 1), to_next(left, -1)
         if last:
             most = call(
                 partial(apply_last, index, slots),
                 f32(matrix.shape),
-                [SMEM, SMEM] + [VMEM] * 4,
-                [pltpu.VMEM((slots, rows, BLOCK), F32), sems],
+                [ANY] + [VMEM] * 4,
+                table + [pltpu.VMEM((slots, rows, BLOCK), F32), sems],
                 flops=pairs * product_flops,
                 out_spec=ANY,
-            )(sources, device, high, low, rh, rl)
+            )(sources, high, low, rh, rl)
             return call(
                 partial(settle, index, slots),
                 f32(matrix.shape),
-                [SMEM, SMEM, ANY, VMEM, VMEM],
+                [SMEM, ANY, VMEM, VMEM],
                 [sems],
                 out_spec=ANY,
-                alias={2: 0},
-            )(sources, device, most, lower, upper)
+                alias={1: 0},
+            )(sources, most, lower, upper)
         selves, self_right, self_left = call(
             partial(carry_self, index, slots),
             (f32((slots, BLOCK, BLOCK)), small, small),
-            [SMEM, SMEM] + [VMEM] * 4,
-            [pltpu.VMEM((PAIR, BLOCK), BF16)] * 4,
+            [ANY] + [VMEM] * 4,
+            table + [pltpu.VMEM((PAIR, BLOCK), BF16)] * 4,
             flops=3 * pairs * product_flops // 2,
-        )(sources, device, *gram, rh, rl)
+        )(sources, *gram, rh, rl)
         own = call(
             partial(apply, slots),
             f32((slots, rows, BLOCK)),
@@ -472,15 +499,16 @@
         part, high, low = call(
             partial(cross_gram, index, slots),
             (f32((row_count, pairs * BLOCK // row_count, BLOCK)), bf16(matrix.shape), bf16(matrix.shape)),
-            [SMEM, SMEM] + [VMEM] * 3,
+            [SMEM] + [VMEM] * 3,
             flops=pairs * product_flops // 4,
-        )(sources, device, own, lower, upper)
+        )(sources, own, lower, upper)
         part, lower_self, upper_self = lax.optimization_barrier((part, lower_self, upper_self))
         mine, selves = call(
             partial(add_up_and_take, index, slots),
             (f32(part.shape), f32((slots, BLOCK, BLOCK))),
-            [SMEM, SMEM] + [VMEM] * 4,
-        )(sources, device, from_rows(part), selves, lower_self, upper_self)
+            [ANY] + [VMEM] * 4,
+            table + [pltpu.VMEM((BLOCK, BLOCK), F32)] * 2,
+        )(sources, from_rows(part), selves, lower_self, upper_self)
         carried = (selves,)
         summed = from_rows(mine)
 

time: 179 us -> 176 us (0.983)
  Pallas kernels: 53.2 us -> 50.1 us
  transfers between devices with their start and end apart: 10 -> 10, of which waited for: 6 -> 6; matrix products, arithmetic and copies ran while one was open for 0% -> 0% of each run, Pallas kernels for 10% -> 9%
where the time goes in v2:
time: 176 us; the launch traced here: 175 us
  blocking collectives  97.7 us (56%)
  Pallas kernels  50.1 us (28%)
  starting transfers between devices  15.2 us (9%)
  waiting for transfers between devices  10.5 us (6%)
    all_to_all x6, blocking collectives, from_rows(): return lax.all_to_all(part, 'row', 0, 0, tiled=True)  97.7 us
    pallas_call x3, Pallas kernels, body(): call(partial(kernel, total_rows, slots), (block, block) + (bf16((pairs,)...  29.5 us
    ppermute x10, starting transfers between devices, to_next(): lax.ppermute(x, 'pair', [(i, (i + by) % count) for i in range(count)])  15.2 us
    ppermute x10, waiting for transfers between devices, to_next(): lax.ppermute(x, 'pair', [(i, (i + by) % count) for i in range(count)])  10.5 us
    pallas_call x2, Pallas kernels, body(): call(partial(carry_self, index, slots), (f32((slots, BLOCK, BLOCK)), smal...  6.02 us
    pallas_call x2, Pallas kernels, body(): call(partial(apply, slots), f32((slots, rows, BLOCK)), [VMEM] * 4 + [ANY]...  3.93 us
  transfers between devices with their start and end apart: 10, of which 6 were waited for; matrix products, arithmetic and copies ran while one was open for 0% of the time, Pallas kernels for 9%

profile of v2, /device:TPU:1, one launch (start us, length us, event | category | flops | bytes accessed | tf_op | source)
XLA Modules:
  0.0 175.4 jit_solution(5081552496097492365)
XLA Ops:
  0.0 1.6 copy-done.1
  3.1 25.1 %all_to_all.30.pieces_ref = f32[16,136,128]{2,1,0:T(8,128)S(1)} all-to-all(f32[16,136,128]{2,1,0:T(8,128)S(1)} %get-tuple-element.52), channel_id=1, replica_groups=mesh['pair'=8,'row'=16] {'row'}, dimensions={0} | all-to-all | bytes 2228224 | tf_op jit(solution)/shard_map/all_to_all | solution.py:429
  28.3 19.0 %all_to_all.31.sum_ref = f32[16,136,128]{2,1,0:T(8,128)S(1)} all-to-all(f32[16,136,128]{2,1,0:T(8,128)S(1)} %shard_map.29), channel_id=1, replica_groups=mesh['pair'=8,'row'=16] {'row'}, dimensions={0} | all-to-all | bytes 2228224 | tf_op jit(solution)/shard_map/all_to_all | solution.py:429
  47.3 9.9 %shard_map.30 = (f32[512,256]{1,0:T(8,128)S(1)}, f32[512,256]{1,0:T(8,128)S(1)}, bf16[2,512,512]{2,1,0:T(8,128)(2,1)S(1)}, bf16[2,512,512]{2,1,0:T(8,128)(2,1)S(...) custom-call(s32[3,32]{1,0:T(4,128)S(1)} %copy-done, f32[16,136,128]{2,1,0:T(8,128)S(1)} %all_to_all.31.sum_ref, ...), custom_call_target="tpu_custom_call" | custom-call | flops 11274289152 | bytes 4000000 | tf_op jit(solution)/shard_map/pallas_call | solution.py:459
  57.2 4.3 %collective-permute-start = (f32[512,256]{1,0:T(8,128)S(1)}, f32[512,256]{1,0:T(8,128)S(1)}, u32[]{:S(2)}, u32[]{:S(2)}) collective-permute-start(f32[512,256]{1,0:T(8,128)S(1)} %get-tuple-element.58), channel_id=1, source_target_pairs={{0,16},{16,32},{32,48},{48,64},{64,80},{80,96},{96,112},{112,0},{1... | collective-permute-start | bytes 1572872 | tf_op jit(solution)/shard_map/ppermute | solution.py:403
  61.5 3.0 %shard_map.31 = (f32[4,256,256]{2,1,0:T(8,128)S(1)}, f32[192,256]{1,0:T(8,128)S(1)}, f32[192,256]{1,0:T(8,128)S(1)}) custom-call(s32[3,32]{1,0:T(4,128)S(1)} %copy-done, bf16[2,512,512]{2,1,0:T(8,128)(2,1)S(1)} %get-tuple-element.55.gh_ref, bf16[2,512,512]{2,1,0:T(8,128)(2,1)S(1)} %get-tuple-element.56.gl_ref, ...), custom_call_target="tpu_custom_call" | custom-call | flops 2415919104 | bytes 4000000 | tf_op jit(solution)/shard_map/pallas_call | solution.py:485
  64.6 1.8 %collective-permute-start.2 = (f32[192,256]{1,0:T(8,128)S(1)}, f32[192,256]{1,0:T(8,128)S(1)}, u32[]{:S(2)}, u32[]{:S(2)}) collective-permute-start(f32[192,256]{1,0:T(8,128)S(1)} %get-tuple-element.63), channel_id=1, source_target_pairs={{0,16},{16,32},{32,48},{48,64},{64,80},{80,96},{96,112},{112,0},{1... | collective-permute-start | bytes 589832 | tf_op jit(solution)/shard_map/ppermute | solution.py:403
  66.4 2.0 %shard_map.32.own_ref = f32[4,512,256]{2,1,0:T(8,128)S(1)} custom-call(bf16[512,1024]{1,0:T(8,128)(2,1)S(1)} %get-tuple-element.50.high_ref, bf16[512,1024]{1,0:T(8,128)(2,1)S(1)} %get-tuple-element.51.low_ref, bf16[2,512,512]{2,1,0:T(8,128)(2,1)S(1)} %get-tuple-element.53.rh_ref, bf16[2,512,512]{2,1,0:T(8,128)(2,1)S(1)} %get-tuple-element.54.rl_ref, ...), custom_call_target="tpu_custom_call" | custom-call | flops 1610612736 | bytes 4000000 | tf_op jit(solution)/shard_map/pallas_call | solution.py:492
  68.3 2.1 %collective-permute-done.1.upper_ref = f32[512,256]{1,0:T(8,128)S(1)} collective-permute-done((f32[512,256]{1,0:T(8,128)S(1)}, f32[512,256]{1,0:T(8,128)S(1)}, u32[]{:S(2)}, u32[]{:S(2)}) %collective-permute-start.1) | collective-permute-done | bytes 524320 | tf_op jit(solution)/shard_map/ppermute | solution.py:403
  72.2 13.3 %all_to_all.32.pieces_ref = f32[16,32,256]{2,1,0:T(8,128)S(1)} all-to-all(f32[16,32,256]{2,1,0:T(8,128)S(1)} %get-tuple-element.65), channel_id=1, replica_groups=mesh['pair'=8,'row'=16] {'row'}, dimensions={0} | all-to-all | bytes 1048576 | tf_op jit(solution)/shard_map/all_to_all | solution.py:429
  86.3 13.4 %all_to_all.33.sum_ref = f32[16,32,256]{2,1,0:T(8,128)S(1)} all-to-all(f32[16,32,256]{2,1,0:T(8,128)S(1)} %get-tuple-element.68), channel_id=1, replica_groups=mesh['pair'=8,'row'=16] {'row'}, dimensions={0} | all-to-all | bytes 1048576 | tf_op jit(solution)/shard_map/all_to_all | solution.py:429
  99.7 9.9 %shard_map.35 = (f32[512,256]{1,0:T(8,128)S(1)}, f32[512,256]{1,0:T(8,128)S(1)}, bf16[2,512,512]{2,1,0:T(8,128)(2,1)S(1)}, bf16[2,512,512]{2,1,0:T(8,128)(2,1)S(...) custom-call(s32[3,32]{1,0:T(4,128)S(1)} %copy-done, f32[16,32,256]{2,1,0:T(8,128)S(1)} %all_to_all.33.sum_ref, ...), custom_call_target="tpu_custom_call" | custom-call | flops 11274289152 | bytes 4000000 | tf_op jit(solution)/shard_map/pallas_call | solution.py:459
  109.5 3.9 %collective-permute-start.4 = (f32[512,256]{1,0:T(8,128)S(1)}, f32[512,256]{1,0:T(8,128)S(1)}, u32[]{:S(2)}, u32[]{:S(2)}) collective-permute-start(f32[512,256]{1,0:T(8,128)S(1)} %get-tuple-element.75), channel_id=1, source_target_pairs={{0,16},{16,32},{32,48},{48,64},{64,80},{80,96},{96,112},{112,0},{1... | collective-permute-start | bytes 1572872 | tf_op jit(solution)/shard_map/ppermute | solution.py:403
  113.5 3.0 %shard_map.36 = (f32[4,256,256]{2,1,0:T(8,128)S(1)}, f32[192,256]{1,0:T(8,128)S(1)}, f32[192,256]{1,0:T(8,128)S(1)}) custom-call(s32[3,32]{1,0:T(4,128)S(1)} %copy-done, bf16[2,512,512]{2,1,0:T(8,128)(2,1)S(1)} %get-tuple-element.72.gh_ref, bf16[2,512,512]{2,1,0:T(8,128)(2,1)S(1)} %get-tuple-element.73.gl_ref, ...), custom_call_target="tpu_custom_call" | custom-call | flops 2415919104 | bytes 4000000 | tf_op jit(solution)/shard_map/pallas_call | solution.py:485
  116.5 1.8 collective-permute-start.6
  118.3 1.9 %shard_map.37.own_ref = f32[4,512,256]{2,1,0:T(8,128)S(1)} custom-call(bf16[512,1024]{1,0:T(8,128)(2,1)S(1)} %get-tuple-element.60.high_ref, bf16[512,1024]{1,0:T(8,128)(2,1)S(1)} %get-tuple-element.61.low_ref, bf16[2,512,512]{2,1,0:T(8,128)(2,1)S(1)} %get-tuple-element.70.rh_ref, bf16[2,512,512]{2,1,0:T(8,128)(2,1)S(1)} %get-tuple-element.71.rl_ref, ...), custom_call_target="tpu_custom_call" | custom-call | flops 1610612736 | bytes 4000000 | tf_op jit(solution)/shard_map/pallas_call | solution.py:492
  120.2 2.2 %collective-permute-done.5.upper_ref = f32[512,256]{1,0:T(8,128)S(1)} collective-permute-done((f32[512,256]{1,0:T(8,128)S(1)}, f32[512,256]{1,0:T(8,128)S(1)}, u32[]{:S(2)}, u32[]{:S(2)}) %collective-permute-start.5) | collective-permute-done | bytes 524320 | tf_op jit(solution)/shard_map/ppermute | solution.py:403
  124.2 13.5 %all_to_all.34.pieces_ref = f32[16,32,256]{2,1,0:T(8,128)S(1)} all-to-all(f32[16,32,256]{2,1,0:T(8,128)S(1)} %get-tuple-element.82), channel_id=1, replica_groups=mesh['pair'=8,'row'=16] {'row'}, dimensions={0} | all-to-all | bytes 1048576 | tf_op jit(solution)/shard_map/all_to_all | solution.py:429
  138.5 13.4 %all_to_all.35.sum_ref = f32[16,32,256]{2,1,0:T(8,128)S(1)} all-to-all(f32[16,32,256]{2,1,0:T(8,128)S(1)} %get-tuple-element.85), channel_id=1, replica_groups=mesh['pair'=8,'row'=16] {'row'}, dimensions={0} | all-to-all | bytes 1048576 | tf_op jit(solution)/shard_map/all_to_all | solution.py:429
  151.8 9.8 %shard_map.40 = (f32[512,256]{1,0:T(8,128)S(1)}, f32[512,256]{1,0:T(8,128)S(1)}, bf16[2,512,512]{2,1,0:T(8,128)(2,1)S(1)}, bf16[2,512,512]{2,1,0:T(8,128)(2,1)S(1)}) custom-call(s32[3,32]{1,0:T(4,128)S(1)} %copy-done, f32[16,32,256]{2,1,0:T(8,128)S(1)} %all_to_all.35.sum_ref, f32[4,256,256]{2,1,0:T(8,128)S(1)} %get-tuple-element.86.self_ref, ...), custom_call_target="tpu_custom_call" | custom-call | flops 11274289152 | bytes 4000000 | tf_op jit(solution)/shard_map/pallas_call | solution.py:459
  161.6 3.4 %collective-permute-start.8 = (f32[512,256]{1,0:T(8,128)S(1)}, f32[512,256]{1,0:T(8,128)S(1)}, u32[]{:S(2)}, u32[]{:S(2)}) collective-permute-start(f32[512,256]{1,0:T(8,128)S(1)} %get-tuple-element.89), channel_id=1, source_target_pairs={{0,16},{16,32},{32,48},{48,64},{64,80},{80,96},{96,112},{112,0},{1... | collective-permute-start | bytes 1572872 | tf_op jit(solution)/shard_map/ppermute | solution.py:403
  165.0 3.0 %shard_map.41.most_ref = f32[512,1024]{1,0:T(8,128)} custom-call(s32[3,32]{1,0:T(4,128)S(1)} %copy-done, bf16[512,1024]{1,0:T(8,128)(2,1)S(1)} %get-tuple-element.77.high_ref, bf16[512,1024]{1,0:T(8,128)(2,1)S(1)} %get-tuple-element.78.low_ref, bf16[2,512,512]{2,1,0:T(8,128)(2,1)S(1)} %get-tuple-element.87.rh_ref, ...), custom_call_target="tpu_custom_call" | custom-call | flops 1610612736 | bytes 4000000 | tf_op jit(solution)/shard_map/pallas_call | solution.py:469
  168.0 3.1 %collective-permute-done.8.lower_ref = f32[512,256]{1,0:T(8,128)S(1)} collective-permute-done((f32[512,256]{1,0:T(8,128)S(1)}, f32[512,256]{1,0:T(8,128)S(1)}, u32[]{:S(2)}, u32[]{:S(2)}) %collective-permute-start.8) | collective-permute-done | bytes 524320 | tf_op jit(solution)/shard_map/ppermute | solution.py:403
  171.1 2.5 %collective-permute-done.9.upper_ref = f32[512,256]{1,0:T(8,128)S(1)} collective-permute-done((f32[512,256]{1,0:T(8,128)S(1)}, f32[512,256]{1,0:T(8,128)S(1)}, u32[]{:S(2)}, u32[]{:S(2)}) %collective-permute-start.9) | collective-permute-done | bytes 524320 | tf_op jit(solution)/shard_map/ppermute | solution.py:403
  (21 shorter events, 8.3 us)
Async XLA Ops:
  0.0 1.6 copy-start.1
  28.2 19.1 %copy-start = (s32[3,32]{1,0:T(4,128)S(1)}, s32[3,32]{1,0:T(4,128)}, u32[]{:S(2)}) copy-start(s32[3,32]{1,0:T(4,128)} %src_ref.2) | copy-start | bytes 1156
  57.2 11.1 %collective-permute-start = (f32[512,256]{1,0:T(8,128)S(1)}, f32[512,256]{1,0:T(8,128)S(1)}, u32[]{:S(2)}, u32[]{:S(2)}) collective-permute-start(f32[512,256]{1,0:T(8,128)S(1)} %get-tuple-element.58), channel_id=1, source_target_pairs={{0,16},{16,32},{32,48},{48,64},{64,80},{80,96},{96,112},{112,0},{1... | collective-permute-start | bytes 1572872 | tf_op jit(solution)/shard_map/ppermute | solution.py:403
  61.5 8.9 %collective-permute-start.1 = (f32[512,256]{1,0:T(8,128)S(1)}, f32[512,256]{1,0:T(8,128)S(1)}, u32[]{:S(2)}, u32[]{:S(2)}) collective-permute-start(f32[512,256]{1,0:T(8,128)S(1)} %get-tuple-element.59), channel_id=1, source_target_pairs={{0,112},{16,0},{32,16},{48,32},{64,48},{80,64},{96,80},{112,96},{1... | collective-permute-start | bytes 1572872 | tf_op jit(solution)/shard_map/ppermute | solution.py:403
  64.6 7.4 %collective-permute-start.2 = (f32[192,256]{1,0:T(8,128)S(1)}, f32[192,256]{1,0:T(8,128)S(1)}, u32[]{:S(2)}, u32[]{:S(2)}) collective-permute-start(f32[192,256]{1,0:T(8,128)S(1)} %get-tuple-element.63), channel_id=1, source_target_pairs={{0,16},{16,32},{32,48},{48,64},{64,80},{80,96},{96,112},{112,0},{1... | collective-permute-start | bytes 589832 | tf_op jit(solution)/shard_map/ppermute | solution.py:403
  66.3 5.9 %collective-permute-start.3 = (f32[192,256]{1,0:T(8,128)S(1)}, f32[192,256]{1,0:T(8,128)S(1)}, u32[]{:S(2)}, u32[]{:S(2)}) collective-permute-start(f32[192,256]{1,0:T(8,128)S(1)} %get-tuple-element.64), channel_id=1, source_target_pairs={{0,112},{16,0},{32,16},{48,32},{64,48},{80,64},{96,80},{112,96},{1... | collective-permute-start | bytes 589832 | tf_op jit(solution)/shard_map/ppermute | solution.py:403
  109.5 10.7 %collective-permute-start.4 = (f32[512,256]{1,0:T(8,128)S(1)}, f32[512,256]{1,0:T(8,128)S(1)}, u32[]{:S(2)}, u32[]{:S(2)}) collective-permute-start(f32[512,256]{1,0:T(8,128)S(1)} %get-tuple-element.75), channel_id=1, source_target_pairs={{0,16},{16,32},{32,48},{48,64},{64,80},{80,96},{96,112},{112,0},{1... | collective-permute-start | bytes 1572872 | tf_op jit(solution)/shard_map/ppermute | solution.py:403
  113.5 8.9 %collective-permute-start.5 = (f32[512,256]{1,0:T(8,128)S(1)}, f32[512,256]{1,0:T(8,128)S(1)}, u32[]{:S(2)}, u32[]{:S(2)}) collective-permute-start(f32[512,256]{1,0:T(8,128)S(1)} %get-tuple-element.76), channel_id=1, source_target_pairs={{0,112},{16,0},{32,16},{48,32},{64,48},{80,64},{96,80},{112,96},{1... | collective-permute-start | bytes 1572872 | tf_op jit(solution)/shard_map/ppermute | solution.py:403
  116.5 7.4 %collective-permute-start.6 = (f32[192,256]{1,0:T(8,128)S(1)}, f32[192,256]{1,0:T(8,128)S(1)}, u32[]{:S(2)}, u32[]{:S(2)}) collective-permute-start(f32[192,256]{1,0:T(8,128)S(1)} %get-tuple-element.80), channel_id=1, source_target_pairs={{0,16},{16,32},{32,48},{48,64},{64,80},{80,96},{96,112},{112,0},{1... | collective-permute-start | bytes 589832 | tf_op jit(solution)/shard_map/ppermute | solution.py:403
  118.3 5.9 %collective-permute-start.7 = (f32[192,256]{1,0:T(8,128)S(1)}, f32[192,256]{1,0:T(8,128)S(1)}, u32[]{:S(2)}, u32[]{:S(2)}) collective-permute-start(f32[192,256]{1,0:T(8,128)S(1)} %get-tuple-element.81), channel_id=1, source_target_pairs={{0,112},{16,0},{32,16},{48,32},{64,48},{80,64},{96,80},{112,96},{1... | collective-permute-start | bytes 589832 | tf_op jit(solution)/shard_map/ppermute | solution.py:403
  161.6 9.5 %collective-permute-start.8 = (f32[512,256]{1,0:T(8,128)S(1)}, f32[512,256]{1,0:T(8,128)S(1)}, u32[]{:S(2)}, u32[]{:S(2)}) collective-permute-start(f32[512,256]{1,0:T(8,128)S(1)} %get-tuple-element.89), channel_id=1, source_target_pairs={{0,16},{16,32},{32,48},{48,64},{64,80},{80,96},{96,112},{112,0},{1... | collective-permute-start | bytes 1572872 | tf_op jit(solution)/shard_map/ppermute | solution.py:403
  165.0 8.6 %collective-permute-start.9 = (f32[512,256]{1,0:T(8,128)S(1)}, f32[512,256]{1,0:T(8,128)S(1)}, u32[]{:S(2)}, u32[]{:S(2)}) collective-permute-start(f32[512,256]{1,0:T(8,128)S(1)} %get-tuple-element.90), channel_id=1, source_target_pairs={{0,112},{16,0},{32,16},{48,32},{64,48},{80,64},{96,80},{112,96},{1... | collective-permute-start | bytes 1572872 | tf_op jit(solution)/shard_map/ppermute | solution.py:403

commit v3 on v2

--- a/solution.py
+++ b/solution.py
@@ -17,7 +17,6 @@
 POLY = (2.25, -2.4375, 1.6875, -0.5625, 0.0625)
 
 VMEM = pl.BlockSpec(memory_space=pltpu.VMEM)
-SMEM = pl.BlockSpec(memory_space=pltpu.SMEM)
 ANY = pl.BlockSpec(memory_space=pl.ANY)
 
 
@@ -62,6 +61,13 @@
 def own_source(src_ref, round_index, slot, slots):
     base = lax.axis_index("pair") * slots
     return src_ref[round_index, base + slot] - base
+
+
+def own_sources(table_ref, round_index, slots):
+    base = lax.axis_index("pair") * slots
+    row = table_ref[pl.ds(round_index, 1), :].astype(F32)
+    lane = lax.broadcasted_iota(jnp.int32, row.shape, 1)
+    return [jnp.sum(jnp.where(lane == base + slot, row, 0.0)).astype(jnp.int32) - base for slot in range(slots)]
 
 
 def leaving(src_ref, round_index, step, slots):
@@ -114,8 +120,7 @@
 def cross_gram(round_index, slots, src_ref, own_ref, lower_ref, upper_ref, part_ref, high_ref, low_ref):
     rows = part_ref.shape[1]
     per = BLOCK // rows
-    for slot in range(slots):
-        offset = own_source(src_ref, round_index, slot, slots)
+    for slot, offset in enumerate(own_sources(src_ref, round_index, slots)):
         high, low = split(picked(offset, slots, own_ref, lower_ref, upper_ref))
         high_ref[:, pl.ds(slot * BLOCK, BLOCK)] = high
         low_ref[:, pl.ds(slot * BLOCK, BLOCK)] = low
@@ -368,7 +373,14 @@
 
 def apply_last(round_index, slots, table_ref, high_ref, low_ref, rh_ref, rl_ref, out_ref, src_ref, sem, own_ref, sems):
     table = fetch(table_ref, src_ref, sem)
-    apply(slots, high_ref, low_ref, rh_ref, rl_ref, None, own_ref)
+
+    @pl.loop(0, slots)
+    def _(slot):
+        pair, half = slot >> 1, slot & 1
+        rows = pl.ds(pl.multiple_of(pair * PAIR, PAIR), PAIR)
+        cols = pl.ds(pl.multiple_of(half * BLOCK, BLOCK), BLOCK)
+        own_ref[slot] = product(high_ref.at[:, rows], low_ref.at[:, rows], rh_ref.at[pair], rl_ref.at[pair], cols)
+
     table.wait()
     offsets = [own_source(src_ref, round_index, slot, slots) for slot in range(slots)]
     for wait in (False, True):
@@ -382,7 +394,7 @@
 
 
 def settle(round_index, slots, src_ref, most_ref, lower_ref, upper_ref, out_ref, sems):
-    offsets = [own_source(src_ref, round_index, slot, slots) for slot in range(slots)]
+    offsets = own_sources(src_ref, round_index, slots)
     for wait in (False, True):
         for slot, offset in enumerate(offsets):
             goal = out_ref.at[:, pl.ds(slot * BLOCK, BLOCK)]
@@ -405,13 +417,14 @@
 
 def add_up(pieces_ref, out_ref):
     total = jnp.sum(pieces_ref[...], axis=0)
-    for chunk in range(out_ref.shape[0]):
+
+    @pl.loop(0, out_ref.shape[0])
+    def _(chunk):
         out_ref[chunk] = total
 
 
 def add_up_and_take(round_index, slots, table_ref, pieces_ref, self_ref, lower_ref, upper_ref,
-                    out_ref, taken_ref, src_ref, sem, lower_full, upper_full):
-    table = fetch(table_ref, src_ref, sem)
+                    out_ref, taken_ref, lower_full, upper_full):
     add_up(pieces_ref, out_ref)
     for packed, full in ((lower_ref, lower_full), (upper_ref, upper_full)):
         full[:LANES, :] = packed[:LANES, :]
@@ -419,9 +432,7 @@
         for half in range(2):
             rows = pl.ds(LANES + half * LANES // 2, LANES // 2)
             full[rows, LANES:] = packed[LANES:, pl.ds(half * LANES, LANES)]
-    table.wait()
-    for slot in range(slots):
-        offset = own_source(src_ref, round_index, slot, slots)
+    for slot, offset in enumerate(own_sources(table_ref, round_index, slots)):
         taken_ref[slot] = picked(offset, slots, self_ref, lower_full, upper_full)
 
 
@@ -477,7 +488,7 @@
             return call(
                 partial(settle, index, slots),
                 f32(matrix.shape),
-                [SMEM, ANY, VMEM, VMEM],
+                [VMEM, ANY, VMEM, VMEM],
                 [sems],
                 out_spec=ANY,
                 alias={1: 0},
@@ -499,15 +510,15 @@
         part, high, low = call(
             partial(cross_gram, index, slots),
             (f32((row_count, pairs * BLOCK // row_count, BLOCK)), bf16(matrix.shape), bf16(matrix.shape)),
-            [SMEM] + [VMEM] * 3,
+            [VMEM] * 4,
             flops=pairs * product_flops // 4,
         )(sources, own, lower, upper)
         part, lower_self, upper_self = lax.optimization_barrier((part, lower_self, upper_self))
         mine, selves = call(
             partial(add_up_and_take, index, slots),
             (f32(part.shape), f32((slots, BLOCK, BLOCK))),
-            [ANY] + [VMEM] * 4,
-            table + [pltpu.VMEM((BLOCK, BLOCK), F32)] * 2,
+            [VMEM] * 5,
+            [pltpu.VMEM((BLOCK, BLOCK), F32)] * 2,
         )(sources, from_rows(part), selves, lower_self, upper_self)
         carried = (selves,)
         summed = from_rows(mine)

time: 176 us -> 175 us (level)
  no operation moved by 1% of the time
where the time goes in v3:
time: 175 us
  blocking collectives  98.1 us (56%)
  Pallas kernels  48.6 us (28%)
  starting transfers between devices  15.1 us (9%)
  waiting for transfers between devices  11 us (6%)
    all_to_all x6, blocking collectives, from_rows(): return lax.all_to_all(part, 'row', 0, 0, tiled=True)  98.1 us
    pallas_call x3, Pallas kernels, body(): call(partial(kernel, total_rows, slots), (block, block) + (bf16((pairs,)...  29.5 us
    ppermute x10, starting transfers between devices, to_next(): lax.ppermute(x, 'pair', [(i, (i + by) % count) for i in range(count)])  15.1 us
    ppermute x10, waiting for transfers between devices, to_next(): lax.ppermute(x, 'pair', [(i, (i + by) % count) for i in range(count)])  11 us
    pallas_call x2, Pallas kernels, body(): call(partial(carry_self, index, slots), (f32((slots, BLOCK, BLOCK)), smal...  6.02 us
    pallas_call x2, Pallas kernels, body(): call(partial(apply, slots), f32((slots, rows, BLOCK)), [VMEM] * 4 + [ANY]...  3.93 us
  transfers between devices with their start and end apart: 10, of which 6 were waited for; matrix products, arithmetic and copies ran while one was open for 0% of the time, Pallas kernels for 9%

profile of v3, /device:TPU:1, one launch (start us, length us, event | category | flops | bytes accessed | tf_op | source)
XLA Modules:
  0.0 174.6 jit_solution(3406429011883533434)
XLA Ops:
  0.0 1.6 copy-done.1
  3.1 25.1 %all_to_all.30.pieces_ref = f32[16,136,128]{2,1,0:T(8,128)S(1)} all-to-all(f32[16,136,128]{2,1,0:T(8,128)S(1)} %get-tuple-element.52), channel_id=1, replica_groups=mesh['pair'=8,'row'=16] {'row'}, dimensions={0} | all-to-all | bytes 2228224 | tf_op jit(solution)/shard_map/all_to_all | solution.py:440
  28.4 19.0 %all_to_all.31.sum_ref = f32[16,136,128]{2,1,0:T(8,128)S(1)} all-to-all(f32[16,136,128]{2,1,0:T(8,128)S(1)} %shard_map.29), channel_id=1, replica_groups=mesh['pair'=8,'row'=16] {'row'}, dimensions={0} | all-to-all | bytes 2228224 | tf_op jit(solution)/shard_map/all_to_all | solution.py:440
  47.4 9.9 %shard_map.30 = (f32[512,256]{1,0:T(8,128)S(1)}, f32[512,256]{1,0:T(8,128)S(1)}, bf16[2,512,512]{2,1,0:T(8,128)(2,1)S(1)}, bf16[2,512,512]{2,1,0:T(8,128)(2,1)S(...) custom-call(s32[3,32]{1,0:T(4,128)S(1)} %copy-done, f32[16,136,128]{2,1,0:T(8,128)S(1)} %all_to_all.31.sum_ref, ...), custom_call_target="tpu_custom_call" | custom-call | flops 11274289152 | bytes 4000000 | tf_op jit(solution)/shard_map/pallas_call | solution.py:470
  57.3 4.3 %collective-permute-start = (f32[512,256]{1,0:T(8,128)S(1)}, f32[512,256]{1,0:T(8,128)S(1)}, u32[]{:S(2)}, u32[]{:S(2)}) collective-permute-start(f32[512,256]{1,0:T(8,128)S(1)} %get-tuple-element.58), channel_id=1, source_target_pairs={{0,16},{16,32},{32,48},{48,64},{64,80},{80,96},{96,112},{112,0},{1... | collective-permute-start | bytes 1572872 | tf_op jit(solution)/shard_map/ppermute | solution.py:415
  61.6 3.0 %shard_map.31 = (f32[4,256,256]{2,1,0:T(8,128)S(1)}, f32[192,256]{1,0:T(8,128)S(1)}, f32[192,256]{1,0:T(8,128)S(1)}) custom-call(s32[3,32]{1,0:T(4,128)S(1)} %copy-done, bf16[2,512,512]{2,1,0:T(8,128)(2,1)S(1)} %get-tuple-element.55.gh_ref, bf16[2,512,512]{2,1,0:T(8,128)(2,1)S(1)} %get-tuple-element.56.gl_ref, ...), custom_call_target="tpu_custom_call" | custom-call | flops 2415919104 | bytes 4000000 | tf_op jit(solution)/shard_map/pallas_call | solution.py:496
  64.6 1.8 %collective-permute-start.2 = (f32[192,256]{1,0:T(8,128)S(1)}, f32[192,256]{1,0:T(8,128)S(1)}, u32[]{:S(2)}, u32[]{:S(2)}) collective-permute-start(f32[192,256]{1,0:T(8,128)S(1)} %get-tuple-element.63), channel_id=1, source_target_pairs={{0,16},{16,32},{32,48},{48,64},{64,80},{80,96},{96,112},{112,0},{1... | collective-permute-start | bytes 589832 | tf_op jit(solution)/shard_map/ppermute | solution.py:415
  66.4 2.0 %shard_map.32.own_ref = f32[4,512,256]{2,1,0:T(8,128)S(1)} custom-call(bf16[512,1024]{1,0:T(8,128)(2,1)S(1)} %get-tuple-element.50.high_ref, bf16[512,1024]{1,0:T(8,128)(2,1)S(1)} %get-tuple-element.51.low_ref, bf16[2,512,512]{2,1,0:T(8,128)(2,1)S(1)} %get-tuple-element.53.rh_ref, bf16[2,512,512]{2,1,0:T(8,128)(2,1)S(1)} %get-tuple-element.54.rl_ref, ...), custom_call_target="tpu_custom_call" | custom-call | flops 1610612736 | bytes 4000000 | tf_op jit(solution)/shard_map/pallas_call | solution.py:503
  68.4 2.1 %collective-permute-done.1.upper_ref = f32[512,256]{1,0:T(8,128)S(1)} collective-permute-done((f32[512,256]{1,0:T(8,128)S(1)}, f32[512,256]{1,0:T(8,128)S(1)}, u32[]{:S(2)}, u32[]{:S(2)}) %collective-permute-start.1) | collective-permute-done | bytes 524320 | tf_op jit(solution)/shard_map/ppermute | solution.py:415
  72.3 13.5 %all_to_all.32.pieces_ref = f32[16,32,256]{2,1,0:T(8,128)S(1)} all-to-all(f32[16,32,256]{2,1,0:T(8,128)S(1)} %get-tuple-element.65), channel_id=1, replica_groups=mesh['pair'=8,'row'=16] {'row'}, dimensions={0} | all-to-all | bytes 1048576 | tf_op jit(solution)/shard_map/all_to_all | solution.py:440
  86.2 13.6 %all_to_all.33.sum_ref = f32[16,32,256]{2,1,0:T(8,128)S(1)} all-to-all(f32[16,32,256]{2,1,0:T(8,128)S(1)} %get-tuple-element.68), channel_id=1, replica_groups=mesh['pair'=8,'row'=16] {'row'}, dimensions={0} | all-to-all | bytes 1048576 | tf_op jit(solution)/shard_map/all_to_all | solution.py:440
  99.8 9.9 %shard_map.35 = (f32[512,256]{1,0:T(8,128)S(1)}, f32[512,256]{1,0:T(8,128)S(1)}, bf16[2,512,512]{2,1,0:T(8,128)(2,1)S(1)}, bf16[2,512,512]{2,1,0:T(8,128)(2,1)S(...) custom-call(s32[3,32]{1,0:T(4,128)S(1)} %copy-done, f32[16,32,256]{2,1,0:T(8,128)S(1)} %all_to_all.33.sum_ref, ...), custom_call_target="tpu_custom_call" | custom-call | flops 11274289152 | bytes 4000000 | tf_op jit(solution)/shard_map/pallas_call | solution.py:470
  109.7 3.7 %collective-permute-start.4 = (f32[512,256]{1,0:T(8,128)S(1)}, f32[512,256]{1,0:T(8,128)S(1)}, u32[]{:S(2)}, u32[]{:S(2)}) collective-permute-start(f32[512,256]{1,0:T(8,128)S(1)} %get-tuple-element.75), channel_id=1, source_target_pairs={{0,16},{16,32},{32,48},{48,64},{64,80},{80,96},{96,112},{112,0},{1... | collective-permute-start | bytes 1572872 | tf_op jit(solution)/shard_map/ppermute | solution.py:415
  113.4 3.0 %shard_map.36 = (f32[4,256,256]{2,1,0:T(8,128)S(1)}, f32[192,256]{1,0:T(8,128)S(1)}, f32[192,256]{1,0:T(8,128)S(1)}) custom-call(s32[3,32]{1,0:T(4,128)S(1)} %copy-done, bf16[2,512,512]{2,1,0:T(8,128)(2,1)S(1)} %get-tuple-element.72.gh_ref, bf16[2,512,512]{2,1,0:T(8,128)(2,1)S(1)} %get-tuple-element.73.gl_ref, ...), custom_call_target="tpu_custom_call" | custom-call | flops 2415919104 | bytes 4000000 | tf_op jit(solution)/shard_map/pallas_call | solution.py:496
  116.5 1.8 %collective-permute-start.6 = (f32[192,256]{1,0:T(8,128)S(1)}, f32[192,256]{1,0:T(8,128)S(1)}, u32[]{:S(2)}, u32[]{:S(2)}) collective-permute-start(f32[192,256]{1,0:T(8,128)S(1)} %get-tuple-element.80), channel_id=1, source_target_pairs={{0,16},{16,32},{32,48},{48,64},{64,80},{80,96},{96,112},{112,0},{1... | collective-permute-start | bytes 589832 | tf_op jit(solution)/shard_map/ppermute | solution.py:415
  118.2 1.9 %shard_map.37.own_ref = f32[4,512,256]{2,1,0:T(8,128)S(1)} custom-call(bf16[512,1024]{1,0:T(8,128)(2,1)S(1)} %get-tuple-element.60.high_ref, bf16[512,1024]{1,0:T(8,128)(2,1)S(1)} %get-tuple-element.61.low_ref, bf16[2,512,512]{2,1,0:T(8,128)(2,1)S(1)} %get-tuple-element.70.rh_ref, bf16[2,512,512]{2,1,0:T(8,128)(2,1)S(1)} %get-tuple-element.71.rl_ref, ...), custom_call_target="tpu_custom_call" | custom-call | flops 1610612736 | bytes 4000000 | tf_op jit(solution)/shard_map/pallas_call | solution.py:503
  120.2 2.2 %collective-permute-done.5.upper_ref = f32[512,256]{1,0:T(8,128)S(1)} collective-permute-done((f32[512,256]{1,0:T(8,128)S(1)}, f32[512,256]{1,0:T(8,128)S(1)}, u32[]{:S(2)}, u32[]{:S(2)}) %collective-permute-start.5) | collective-permute-done | bytes 524320 | tf_op jit(solution)/shard_map/ppermute | solution.py:415
  124.1 13.5 %all_to_all.34.pieces_ref = f32[16,32,256]{2,1,0:T(8,128)S(1)} all-to-all(f32[16,32,256]{2,1,0:T(8,128)S(1)} %get-tuple-element.82), channel_id=1, replica_groups=mesh['pair'=8,'row'=16] {'row'}, dimensions={0} | all-to-all | bytes 1048576 | tf_op jit(solution)/shard_map/all_to_all | solution.py:440
  138.1 13.4 %all_to_all.35.sum_ref = f32[16,32,256]{2,1,0:T(8,128)S(1)} all-to-all(f32[16,32,256]{2,1,0:T(8,128)S(1)} %get-tuple-element.85), channel_id=1, replica_groups=mesh['pair'=8,'row'=16] {'row'}, dimensions={0} | all-to-all | bytes 1048576 | tf_op jit(solution)/shard_map/all_to_all | solution.py:440
  151.5 9.8 %shard_map.40 = (f32[512,256]{1,0:T(8,128)S(1)}, f32[512,256]{1,0:T(8,128)S(1)}, bf16[2,512,512]{2,1,0:T(8,128)(2,1)S(1)}, bf16[2,512,512]{2,1,0:T(8,128)(2,1)S(1)}) custom-call(s32[3,32]{1,0:T(4,128)S(1)} %copy-done, f32[16,32,256]{2,1,0:T(8,128)S(1)} %all_to_all.35.sum_ref, f32[4,256,256]{2,1,0:T(8,128)S(1)} %get-tuple-element.86.self_ref, ...), custom_call_target="tpu_custom_call" | custom-call | flops 11274289152 | bytes 4000000 | tf_op jit(solution)/shard_map/pallas_call | solution.py:470
  161.2 3.5 %collective-permute-start.8 = (f32[512,256]{1,0:T(8,128)S(1)}, f32[512,256]{1,0:T(8,128)S(1)}, u32[]{:S(2)}, u32[]{:S(2)}) collective-permute-start(f32[512,256]{1,0:T(8,128)S(1)} %get-tuple-element.89), channel_id=1, source_target_pairs={{0,16},{16,32},{32,48},{48,64},{64,80},{80,96},{96,112},{112,0},{1... | collective-permute-start | bytes 1572872 | tf_op jit(solution)/shard_map/ppermute | solution.py:415
  164.7 3.4 %shard_map.41.most_ref = f32[512,1024]{1,0:T(8,128)} custom-call(s32[3,32]{1,0:T(4,128)S(1)} %copy-done, bf16[512,1024]{1,0:T(8,128)(2,1)S(1)} %get-tuple-element.77.high_ref, bf16[512,1024]{1,0:T(8,128)(2,1)S(1)} %get-tuple-element.78.low_ref, bf16[2,512,512]{2,1,0:T(8,128)(2,1)S(1)} %get-tuple-element.87.rh_ref, ...), custom_call_target="tpu_custom_call" | custom-call | flops 1610612736 | bytes 4000000 | tf_op jit(solution)/shard_map/pallas_call | solution.py:480
  168.1 2.8 %collective-permute-done.8.lower_ref = f32[512,256]{1,0:T(8,128)S(1)} collective-permute-done((f32[512,256]{1,0:T(8,128)S(1)}, f32[512,256]{1,0:T(8,128)S(1)}, u32[]{:S(2)}, u32[]{:S(2)}) %collective-permute-start.8) | collective-permute-done | bytes 524320 | tf_op jit(solution)/shard_map/ppermute | solution.py:415
  170.8 2.5 %collective-permute-done.9.upper_ref = f32[512,256]{1,0:T(8,128)S(1)} collective-permute-done((f32[512,256]{1,0:T(8,128)S(1)}, f32[512,256]{1,0:T(8,128)S(1)}, u32[]{:S(2)}, u32[]{:S(2)}) %collective-permute-start.9) | collective-permute-done | bytes 524320 | tf_op jit(solution)/shard_map/ppermute | solution.py:415
  (21 shorter events, 7.3 us)
Async XLA Ops:
  0.0 1.6 copy-start.1
  28.2 19.1 %copy-start = (s32[3,32]{1,0:T(4,128)S(1)}, s32[3,32]{1,0:T(4,128)}, u32[]{:S(2)}) copy-start(s32[3,32]{1,0:T(4,128)} %src_ref.2) | copy-start | bytes 1156
  57.3 11.1 %collective-permute-start = (f32[512,256]{1,0:T(8,128)S(1)}, f32[512,256]{1,0:T(8,128)S(1)}, u32[]{:S(2)}, u32[]{:S(2)}) collective-permute-start(f32[512,256]{1,0:T(8,128)S(1)} %get-tuple-element.58), channel_id=1, source_target_pairs={{0,16},{16,32},{32,48},{48,64},{64,80},{80,96},{96,112},{112,0},{1... | collective-permute-start | bytes 1572872 | tf_op jit(solution)/shard_map/ppermute | solution.py:415
  61.6 8.9 %collective-permute-start.1 = (f32[512,256]{1,0:T(8,128)S(1)}, f32[512,256]{1,0:T(8,128)S(1)}, u32[]{:S(2)}, u32[]{:S(2)}) collective-permute-start(f32[512,256]{1,0:T(8,128)S(1)} %get-tuple-element.59), channel_id=1, source_target_pairs={{0,112},{16,0},{32,16},{48,32},{64,48},{80,64},{96,80},{112,96},{1... | collective-permute-start | bytes 1572872 | tf_op jit(solution)/shard_map/ppermute | solution.py:415
  64.6 6.9 %collective-permute-start.2 = (f32[192,256]{1,0:T(8,128)S(1)}, f32[192,256]{1,0:T(8,128)S(1)}, u32[]{:S(2)}, u32[]{:S(2)}) collective-permute-start(f32[192,256]{1,0:T(8,128)S(1)} %get-tuple-element.63), channel_id=1, source_target_pairs={{0,16},{16,32},{32,48},{48,64},{64,80},{80,96},{96,112},{112,0},{1... | collective-permute-start | bytes 589832 | tf_op jit(solution)/shard_map/ppermute | solution.py:415
  66.4 5.9 %collective-permute-start.3 = (f32[192,256]{1,0:T(8,128)S(1)}, f32[192,256]{1,0:T(8,128)S(1)}, u32[]{:S(2)}, u32[]{:S(2)}) collective-permute-start(f32[192,256]{1,0:T(8,128)S(1)} %get-tuple-element.64), channel_id=1, source_target_pairs={{0,112},{16,0},{32,16},{48,32},{64,48},{80,64},{96,80},{112,96},{1... | collective-permute-start | bytes 589832 | tf_op jit(solution)/shard_map/ppermute | solution.py:415
  109.7 10.5 %collective-permute-start.4 = (f32[512,256]{1,0:T(8,128)S(1)}, f32[512,256]{1,0:T(8,128)S(1)}, u32[]{:S(2)}, u32[]{:S(2)}) collective-permute-start(f32[512,256]{1,0:T(8,128)S(1)} %get-tuple-element.75), channel_id=1, source_target_pairs={{0,16},{16,32},{32,48},{48,64},{64,80},{80,96},{96,112},{112,0},{1... | collective-permute-start | bytes 1572872 | tf_op jit(solution)/shard_map/ppermute | solution.py:415
  113.4 8.9 %collective-permute-start.5 = (f32[512,256]{1,0:T(8,128)S(1)}, f32[512,256]{1,0:T(8,128)S(1)}, u32[]{:S(2)}, u32[]{:S(2)}) collective-permute-start(f32[512,256]{1,0:T(8,128)S(1)} %get-tuple-element.76), channel_id=1, source_target_pairs={{0,112},{16,0},{32,16},{48,32},{64,48},{80,64},{96,80},{112,96},{1... | collective-permute-start | bytes 1572872 | tf_op jit(solution)/shard_map/ppermute | solution.py:415
  116.5 6.9 %collective-permute-start.6 = (f32[192,256]{1,0:T(8,128)S(1)}, f32[192,256]{1,0:T(8,128)S(1)}, u32[]{:S(2)}, u32[]{:S(2)}) collective-permute-start(f32[192,256]{1,0:T(8,128)S(1)} %get-tuple-element.80), channel_id=1, source_target_pairs={{0,16},{16,32},{32,48},{48,64},{64,80},{80,96},{96,112},{112,0},{1... | collective-permute-start | bytes 589832 | tf_op jit(solution)/shard_map/ppermute | solution.py:415
  118.2 5.9 %collective-permute-start.7 = (f32[192,256]{1,0:T(8,128)S(1)}, f32[192,256]{1,0:T(8,128)S(1)}, u32[]{:S(2)}, u32[]{:S(2)}) collective-permute-start(f32[192,256]{1,0:T(8,128)S(1)} %get-tuple-element.81), channel_id=1, source_target_pairs={{0,112},{16,0},{32,16},{48,32},{64,48},{80,64},{96,80},{112,96},{1... | collective-permute-start | bytes 589832 | tf_op jit(solution)/shard_map/ppermute | solution.py:415
  161.2 9.6 %collective-permute-start.8 = (f32[512,256]{1,0:T(8,128)S(1)}, f32[512,256]{1,0:T(8,128)S(1)}, u32[]{:S(2)}, u32[]{:S(2)}) collective-permute-start(f32[512,256]{1,0:T(8,128)S(1)} %get-tuple-element.89), channel_id=1, source_target_pairs={{0,16},{16,32},{32,48},{48,64},{64,80},{80,96},{96,112},{112,0},{1... | collective-permute-start | bytes 1572872 | tf_op jit(solution)/shard_map/ppermute | solution.py:415
  164.7 8.6 %collective-permute-start.9 = (f32[512,256]{1,0:T(8,128)S(1)}, f32[512,256]{1,0:T(8,128)S(1)}, u32[]{:S(2)}, u32[]{:S(2)}) collective-permute-start(f32[512,256]{1,0:T(8,128)S(1)} %get-tuple-element.90), channel_id=1, source_target_pairs={{0,112},{16,0},{32,16},{48,32},{64,48},{80,64},{96,80},{112,96},{1... | collective-permute-start | bytes 1572872 | tf_op jit(solution)/shard_map/ppermute | solution.py:415

commit v4 on v3

--- a/solution.py
+++ b/solution.py
@@ -418,7 +418,7 @@
 def add_up(pieces_ref, out_ref):
     total = jnp.sum(pieces_ref[...], axis=0)
 
-    @pl.loop(0, out_ref.shape[0])
+    @pl.loop(0, out_ref.shape[0], unroll=4)
     def _(chunk):
         out_ref[chunk] = total
 

time: 175 us -> 175 us (level)
  no operation moved by 1% of the time
where the time goes in v4:
time: 175 us; the launch traced here: 174 us
  blocking collectives  98.1 us (56%)
  Pallas kernels  48.4 us (28%)
  starting transfers between devices  15.1 us (9%)
  waiting for transfers between devices  11 us (6%)
    all_to_all x6, blocking collectives, from_rows(): return lax.all_to_all(part, 'row', 0, 0, tiled=True)  98.1 us
    pallas_call x3, Pallas kernels, body(): call(partial(kernel, total_rows, slots), (block, block) + (bf16((pairs,)...  29.5 us
    ppermute x10, starting transfers between devices, to_next(): lax.ppermute(x, 'pair', [(i, (i + by) % count) for i in range(count)])  15.1 us
    ppermute x10, waiting for transfers between devices, to_next(): lax.ppermute(x, 'pair', [(i, (i + by) % count) for i in range(count)])  11 us
    pallas_call x2, Pallas kernels, body(): call(partial(carry_self, index, slots), (f32((slots, BLOCK, BLOCK)), smal...  6.01 us
    pallas_call x2, Pallas kernels, body(): call(partial(apply, slots), f32((slots, rows, BLOCK)), [VMEM] * 4 + [ANY]...  3.93 us
  transfers between devices with their start and end apart: 10, of which 6 were waited for; matrix products, arithmetic and copies ran while one was open for 0% of the time, Pallas kernels for 9%

profile of v4, /device:TPU:1, one launch (start us, length us, event | category | flops | bytes accessed | tf_op | source)
XLA Modules:
  0.0 174.5 jit_solution(4116968183290523471)
XLA Ops:
  0.0 1.6 copy-done.1
  3.1 25.1 %all_to_all.30.pieces_ref = f32[16,136,128]{2,1,0:T(8,128)S(1)} all-to-all(f32[16,136,128]{2,1,0:T(8,128)S(1)} %get-tuple-element.52), channel_id=1, replica_groups=mesh['pair'=8,'row'=16] {'row'}, dimensions={0} | all-to-all | bytes 2228224 | tf_op jit(solution)/shard_map/all_to_all | solution.py:440
  28.4 19.0 %all_to_all.31.sum_ref = f32[16,136,128]{2,1,0:T(8,128)S(1)} all-to-all(f32[16,136,128]{2,1,0:T(8,128)S(1)} %shard_map.29), channel_id=1, replica_groups=mesh['pair'=8,'row'=16] {'row'}, dimensions={0} | all-to-all | bytes 2228224 | tf_op jit(solution)/shard_map/all_to_all | solution.py:440
  47.4 9.9 %shard_map.30 = (f32[512,256]{1,0:T(8,128)S(1)}, f32[512,256]{1,0:T(8,128)S(1)}, bf16[2,512,512]{2,1,0:T(8,128)(2,1)S(1)}, bf16[2,512,512]{2,1,0:T(8,128)(2,1)S(...) custom-call(s32[3,32]{1,0:T(4,128)S(1)} %copy-done, f32[16,136,128]{2,1,0:T(8,128)S(1)} %all_to_all.31.sum_ref, ...), custom_call_target="tpu_custom_call" | custom-call | flops 11274289152 | bytes 4000000 | tf_op jit(solution)/shard_map/pallas_call | solution.py:470
  57.3 4.3 %collective-permute-start = (f32[512,256]{1,0:T(8,128)S(1)}, f32[512,256]{1,0:T(8,128)S(1)}, u32[]{:S(2)}, u32[]{:S(2)}) collective-permute-start(f32[512,256]{1,0:T(8,128)S(1)} %get-tuple-element.58), channel_id=1, source_target_pairs={{0,16},{16,32},{32,48},{48,64},{64,80},{80,96},{96,112},{112,0},{1... | collective-permute-start | bytes 1572872 | tf_op jit(solution)/shard_map/ppermute | solution.py:415
  61.6 3.0 %shard_map.31 = (f32[4,256,256]{2,1,0:T(8,128)S(1)}, f32[192,256]{1,0:T(8,128)S(1)}, f32[192,256]{1,0:T(8,128)S(1)}) custom-call(s32[3,32]{1,0:T(4,128)S(1)} %copy-done, bf16[2,512,512]{2,1,0:T(8,128)(2,1)S(1)} %get-tuple-element.55.gh_ref, bf16[2,512,512]{2,1,0:T(8,128)(2,1)S(1)} %get-tuple-element.56.gl_ref, ...), custom_call_target="tpu_custom_call" | custom-call | flops 2415919104 | bytes 4000000 | tf_op jit(solution)/shard_map/pallas_call | solution.py:496
  64.6 1.8 %collective-permute-start.2 = (f32[192,256]{1,0:T(8,128)S(1)}, f32[192,256]{1,0:T(8,128)S(1)}, u32[]{:S(2)}, u32[]{:S(2)}) collective-permute-start(f32[192,256]{1,0:T(8,128)S(1)} %get-tuple-element.63), channel_id=1, source_target_pairs={{0,16},{16,32},{32,48},{48,64},{64,80},{80,96},{96,112},{112,0},{1... | collective-permute-start | bytes 589832 | tf_op jit(solution)/shard_map/ppermute | solution.py:415
  66.4 2.0 %shard_map.32.own_ref = f32[4,512,256]{2,1,0:T(8,128)S(1)} custom-call(bf16[512,1024]{1,0:T(8,128)(2,1)S(1)} %get-tuple-element.50.high_ref, bf16[512,1024]{1,0:T(8,128)(2,1)S(1)} %get-tuple-element.51.low_ref, bf16[2,512,512]{2,1,0:T(8,128)(2,1)S(1)} %get-tuple-element.53.rh_ref, bf16[2,512,512]{2,1,0:T(8,128)(2,1)S(1)} %get-tuple-element.54.rl_ref, ...), custom_call_target="tpu_custom_call" | custom-call | flops 1610612736 | bytes 4000000 | tf_op jit(solution)/shard_map/pallas_call | solution.py:503
  68.4 2.1 %collective-permute-done.1.upper_ref = f32[512,256]{1,0:T(8,128)S(1)} collective-permute-done((f32[512,256]{1,0:T(8,128)S(1)}, f32[512,256]{1,0:T(8,128)S(1)}, u32[]{:S(2)}, u32[]{:S(2)}) %collective-permute-start.1) | collective-permute-done | bytes 524320 | tf_op jit(solution)/shard_map/ppermute | solution.py:415
  72.3 13.5 %all_to_all.32.pieces_ref = f32[16,32,256]{2,1,0:T(8,128)S(1)} all-to-all(f32[16,32,256]{2,1,0:T(8,128)S(1)} %get-tuple-element.65), channel_id=1, replica_groups=mesh['pair'=8,'row'=16] {'row'}, dimensions={0} | all-to-all | bytes 1048576 | tf_op jit(solution)/shard_map/all_to_all | solution.py:440
  86.1 13.6 %all_to_all.33.sum_ref = f32[16,32,256]{2,1,0:T(8,128)S(1)} all-to-all(f32[16,32,256]{2,1,0:T(8,128)S(1)} %get-tuple-element.68), channel_id=1, replica_groups=mesh['pair'=8,'row'=16] {'row'}, dimensions={0} | all-to-all | bytes 1048576 | tf_op jit(solution)/shard_map/all_to_all | solution.py:440
  99.7 9.9 %shard_map.35 = (f32[512,256]{1,0:T(8,128)S(1)}, f32[512,256]{1,0:T(8,128)S(1)}, bf16[2,512,512]{2,1,0:T(8,128)(2,1)S(1)}, bf16[2,512,512]{2,1,0:T(8,128)(2,1)S(...) custom-call(s32[3,32]{1,0:T(4,128)S(1)} %copy-done, f32[16,32,256]{2,1,0:T(8,128)S(1)} %all_to_all.33.sum_ref, ...), custom_call_target="tpu_custom_call" | custom-call | flops 11274289152 | bytes 4000000 | tf_op jit(solution)/shard_map/pallas_call | solution.py:470
  109.6 3.7 %collective-permute-start.4 = (f32[512,256]{1,0:T(8,128)S(1)}, f32[512,256]{1,0:T(8,128)S(1)}, u32[]{:S(2)}, u32[]{:S(2)}) collective-permute-start(f32[512,256]{1,0:T(8,128)S(1)} %get-tuple-element.75), channel_id=1, source_target_pairs={{0,16},{16,32},{32,48},{48,64},{64,80},{80,96},{96,112},{112,0},{1... | collective-permute-start | bytes 1572872 | tf_op jit(solution)/shard_map/ppermute | solution.py:415
  113.3 3.0 %shard_map.36 = (f32[4,256,256]{2,1,0:T(8,128)S(1)}, f32[192,256]{1,0:T(8,128)S(1)}, f32[192,256]{1,0:T(8,128)S(1)}) custom-call(s32[3,32]{1,0:T(4,128)S(1)} %copy-done, bf16[2,512,512]{2,1,0:T(8,128)(2,1)S(1)} %get-tuple-element.72.gh_ref, bf16[2,512,512]{2,1,0:T(8,128)(2,1)S(1)} %get-tuple-element.73.gl_ref, ...), custom_call_target="tpu_custom_call" | custom-call | flops 2415919104 | bytes 4000000 | tf_op jit(solution)/shard_map/pallas_call | solution.py:496
  116.4 1.8 %collective-permute-start.6 = (f32[192,256]{1,0:T(8,128)S(1)}, f32[192,256]{1,0:T(8,128)S(1)}, u32[]{:S(2)}, u32[]{:S(2)}) collective-permute-start(f32[192,256]{1,0:T(8,128)S(1)} %get-tuple-element.80), channel_id=1, source_target_pairs={{0,16},{16,32},{32,48},{48,64},{64,80},{80,96},{96,112},{112,0},{1... | collective-permute-start | bytes 589832 | tf_op jit(solution)/shard_map/ppermute | solution.py:415
  118.1 1.9 %shard_map.37.own_ref = f32[4,512,256]{2,1,0:T(8,128)S(1)} custom-call(bf16[512,1024]{1,0:T(8,128)(2,1)S(1)} %get-tuple-element.60.high_ref, bf16[512,1024]{1,0:T(8,128)(2,1)S(1)} %get-tuple-element.61.low_ref, bf16[2,512,512]{2,1,0:T(8,128)(2,1)S(1)} %get-tuple-element.70.rh_ref, bf16[2,512,512]{2,1,0:T(8,128)(2,1)S(1)} %get-tuple-element.71.rl_ref, ...), custom_call_target="tpu_custom_call" | custom-call | flops 1610612736 | bytes 4000000 | tf_op jit(solution)/shard_map/pallas_call | solution.py:503
  120.1 2.2 %collective-permute-done.5.upper_ref = f32[512,256]{1,0:T(8,128)S(1)} collective-permute-done((f32[512,256]{1,0:T(8,128)S(1)}, f32[512,256]{1,0:T(8,128)S(1)}, u32[]{:S(2)}, u32[]{:S(2)}) %collective-permute-start.5) | collective-permute-done | bytes 524320 | tf_op jit(solution)/shard_map/ppermute | solution.py:415
  124.0 13.5 %all_to_all.34.pieces_ref = f32[16,32,256]{2,1,0:T(8,128)S(1)} all-to-all(f32[16,32,256]{2,1,0:T(8,128)S(1)} %get-tuple-element.82), channel_id=1, replica_groups=mesh['pair'=8,'row'=16] {'row'}, dimensions={0} | all-to-all | bytes 1048576 | tf_op jit(solution)/shard_map/all_to_all | solution.py:440
  137.9 13.4 %all_to_all.35.sum_ref = f32[16,32,256]{2,1,0:T(8,128)S(1)} all-to-all(f32[16,32,256]{2,1,0:T(8,128)S(1)} %get-tuple-element.85), channel_id=1, replica_groups=mesh['pair'=8,'row'=16] {'row'}, dimensions={0} | all-to-all | bytes 1048576 | tf_op jit(solution)/shard_map/all_to_all | solution.py:440
  151.3 9.8 %shard_map.40 = (f32[512,256]{1,0:T(8,128)S(1)}, f32[512,256]{1,0:T(8,128)S(1)}, bf16[2,512,512]{2,1,0:T(8,128)(2,1)S(1)}, bf16[2,512,512]{2,1,0:T(8,128)(2,1)S(1)}) custom-call(s32[3,32]{1,0:T(4,128)S(1)} %copy-done, f32[16,32,256]{2,1,0:T(8,128)S(1)} %all_to_all.35.sum_ref, f32[4,256,256]{2,1,0:T(8,128)S(1)} %get-tuple-element.86.self_ref, ...), custom_call_target="tpu_custom_call" | custom-call | flops 11274289152 | bytes 4000000 | tf_op jit(solution)/shard_map/pallas_call | solution.py:470
  161.1 3.5 %collective-permute-start.8 = (f32[512,256]{1,0:T(8,128)S(1)}, f32[512,256]{1,0:T(8,128)S(1)}, u32[]{:S(2)}, u32[]{:S(2)}) collective-permute-start(f32[512,256]{1,0:T(8,128)S(1)} %get-tuple-element.89), channel_id=1, source_target_pairs={{0,16},{16,32},{32,48},{48,64},{64,80},{80,96},{96,112},{112,0},{1... | collective-permute-start | bytes 1572872 | tf_op jit(solution)/shard_map/ppermute | solution.py:415
  164.6 3.4 %shard_map.41.most_ref = f32[512,1024]{1,0:T(8,128)} custom-call(s32[3,32]{1,0:T(4,128)S(1)} %copy-done, bf16[512,1024]{1,0:T(8,128)(2,1)S(1)} %get-tuple-element.77.high_ref, bf16[512,1024]{1,0:T(8,128)(2,1)S(1)} %get-tuple-element.78.low_ref, bf16[2,512,512]{2,1,0:T(8,128)(2,1)S(1)} %get-tuple-element.87.rh_ref, ...), custom_call_target="tpu_custom_call" | custom-call | flops 1610612736 | bytes 4000000 | tf_op jit(solution)/shard_map/pallas_call | solution.py:480
  167.9 2.8 %collective-permute-done.8.lower_ref = f32[512,256]{1,0:T(8,128)S(1)} collective-permute-done((f32[512,256]{1,0:T(8,128)S(1)}, f32[512,256]{1,0:T(8,128)S(1)}, u32[]{:S(2)}, u32[]{:S(2)}) %collective-permute-start.8) | collective-permute-done | bytes 524320 | tf_op jit(solution)/shard_map/ppermute | solution.py:415
  170.7 2.5 %collective-permute-done.9.upper_ref = f32[512,256]{1,0:T(8,128)S(1)} collective-permute-done((f32[512,256]{1,0:T(8,128)S(1)}, f32[512,256]{1,0:T(8,128)S(1)}, u32[]{:S(2)}, u32[]{:S(2)}) %collective-permute-start.9) | collective-permute-done | bytes 524320 | tf_op jit(solution)/shard_map/ppermute | solution.py:415
  (21 shorter events, 7.2 us)
Async XLA Ops:
  0.0 1.6 copy-start.1
  28.2 19.1 %copy-start = (s32[3,32]{1,0:T(4,128)S(1)}, s32[3,32]{1,0:T(4,128)}, u32[]{:S(2)}) copy-start(s32[3,32]{1,0:T(4,128)} %src_ref.2) | copy-start | bytes 1156
  57.3 11.1 %collective-permute-start = (f32[512,256]{1,0:T(8,128)S(1)}, f32[512,256]{1,0:T(8,128)S(1)}, u32[]{:S(2)}, u32[]{:S(2)}) collective-permute-start(f32[512,256]{1,0:T(8,128)S(1)} %get-tuple-element.58), channel_id=1, source_target_pairs={{0,16},{16,32},{32,48},{48,64},{64,80},{80,96},{96,112},{112,0},{1... | collective-permute-start | bytes 1572872 | tf_op jit(solution)/shard_map/ppermute | solution.py:415
  61.6 8.9 %collective-permute-start.1 = (f32[512,256]{1,0:T(8,128)S(1)}, f32[512,256]{1,0:T(8,128)S(1)}, u32[]{:S(2)}, u32[]{:S(2)}) collective-permute-start(f32[512,256]{1,0:T(8,128)S(1)} %get-tuple-element.59), channel_id=1, source_target_pairs={{0,112},{16,0},{32,16},{48,32},{64,48},{80,64},{96,80},{112,96},{1... | collective-permute-start | bytes 1572872 | tf_op jit(solution)/shard_map/ppermute | solution.py:415
  64.6 6.9 %collective-permute-start.2 = (f32[192,256]{1,0:T(8,128)S(1)}, f32[192,256]{1,0:T(8,128)S(1)}, u32[]{:S(2)}, u32[]{:S(2)}) collective-permute-start(f32[192,256]{1,0:T(8,128)S(1)} %get-tuple-element.63), channel_id=1, source_target_pairs={{0,16},{16,32},{32,48},{48,64},{64,80},{80,96},{96,112},{112,0},{1... | collective-permute-start | bytes 589832 | tf_op jit(solution)/shard_map/ppermute | solution.py:415
  66.3 5.9 %collective-permute-start.3 = (f32[192,256]{1,0:T(8,128)S(1)}, f32[192,256]{1,0:T(8,128)S(1)}, u32[]{:S(2)}, u32[]{:S(2)}) collective-permute-start(f32[192,256]{1,0:T(8,128)S(1)} %get-tuple-element.64), channel_id=1, source_target_pairs={{0,112},{16,0},{32,16},{48,32},{64,48},{80,64},{96,80},{112,96},{1... | collective-permute-start | bytes 589832 | tf_op jit(solution)/shard_map/ppermute | solution.py:415
  109.6 10.5 %collective-permute-start.4 = (f32[512,256]{1,0:T(8,128)S(1)}, f32[512,256]{1,0:T(8,128)S(1)}, u32[]{:S(2)}, u32[]{:S(2)}) collective-permute-start(f32[512,256]{1,0:T(8,128)S(1)} %get-tuple-element.75), channel_id=1, source_target_pairs={{0,16},{16,32},{32,48},{48,64},{64,80},{80,96},{96,112},{112,0},{1... | collective-permute-start | bytes 1572872 | tf_op jit(solution)/shard_map/ppermute | solution.py:415
  113.3 8.9 %collective-permute-start.5 = (f32[512,256]{1,0:T(8,128)S(1)}, f32[512,256]{1,0:T(8,128)S(1)}, u32[]{:S(2)}, u32[]{:S(2)}) collective-permute-start(f32[512,256]{1,0:T(8,128)S(1)} %get-tuple-element.76), channel_id=1, source_target_pairs={{0,112},{16,0},{32,16},{48,32},{64,48},{80,64},{96,80},{112,96},{1... | collective-permute-start | bytes 1572872 | tf_op jit(solution)/shard_map/ppermute | solution.py:415
  116.4 6.9 %collective-permute-start.6 = (f32[192,256]{1,0:T(8,128)S(1)}, f32[192,256]{1,0:T(8,128)S(1)}, u32[]{:S(2)}, u32[]{:S(2)}) collective-permute-start(f32[192,256]{1,0:T(8,128)S(1)} %get-tuple-element.80), channel_id=1, source_target_pairs={{0,16},{16,32},{32,48},{48,64},{64,80},{80,96},{96,112},{112,0},{1... | collective-permute-start | bytes 589832 | tf_op jit(solution)/shard_map/ppermute | solution.py:415
  118.1 5.9 %collective-permute-start.7 = (f32[192,256]{1,0:T(8,128)S(1)}, f32[192,256]{1,0:T(8,128)S(1)}, u32[]{:S(2)}, u32[]{:S(2)}) collective-permute-start(f32[192,256]{1,0:T(8,128)S(1)} %get-tuple-element.81), channel_id=1, source_target_pairs={{0,112},{16,0},{32,16},{48,32},{64,48},{80,64},{96,80},{112,96},{1... | collective-permute-start | bytes 589832 | tf_op jit(solution)/shard_map/ppermute | solution.py:415
  161.1 9.6 %collective-permute-start.8 = (f32[512,256]{1,0:T(8,128)S(1)}, f32[512,256]{1,0:T(8,128)S(1)}, u32[]{:S(2)}, u32[]{:S(2)}) collective-permute-start(f32[512,256]{1,0:T(8,128)S(1)} %get-tuple-element.89), channel_id=1, source_target_pairs={{0,16},{16,32},{32,48},{48,64},{64,80},{80,96},{96,112},{112,0},{1... | collective-permute-start | bytes 1572872 | tf_op jit(solution)/shard_map/ppermute | solution.py:415
  164.6 8.6 %collective-permute-start.9 = (f32[512,256]{1,0:T(8,128)S(1)}, f32[512,256]{1,0:T(8,128)S(1)}, u32[]{:S(2)}, u32[]{:S(2)}) collective-permute-start(f32[512,256]{1,0:T(8,128)S(1)} %get-tuple-element.90), channel_id=1, source_target_pairs={{0,112},{16,0},{32,16},{48,32},{64,48},{80,64},{96,80},{112,96},{1... | collective-permute-start | bytes 1572872 | tf_op jit(solution)/shard_map/ppermute | solution.py:415
